TPU v7x, 32 devices: a whole 2x2x4 slice. The times are simulated.
32 devices in a mesh: dp: 8 (over y, x, core), tensor: 4 (over z).
Axes of the slice: x: 2, y: 2, z: 4, core: 2. Of those that a mesh axis runs over, the one named last changes fastest.
Arguments:
- inputs: bfloat16 [24576, 2048], P(('dp', 'tensor')), may hold values from -6 to 6
- seq_offsets: int32 [8, 3], P('dp'), may hold values from 0 to 3072, as said below
- seq_lengths: int32 [8, 3], P('dp'), may hold values from 0 to 3072, as said below
- norm1_gain: float32 [2048], replicated, may hold values from 0.5 to 1.5
- w_qkv: float32 [2048, 3, 2048], P('dp', None, 'tensor'), may hold values from -0.125 to 0.125
- w_gate_out: float32 [2048, 2048], P('dp', 'tensor'), may hold values from -0.125 to 0.125
- w_decay: float32 [2048, 2, 16], P('dp', None, 'tensor'), may hold values from -0.125 to 0.125
- conv_weight: float32 [3, 4, 2048], P(None, None, 'tensor'), may hold values from -3 to 3
- decay_log: float32 [16], P('tensor'), may hold values from -2 to 1
- decay_bias: float32 [16], P('tensor'), may hold values from -10 to -3
- head_norm_gain: float32 [128], replicated, may hold values from 0.5 to 1.5
- w_output: float32 [2048, 2048], P('dp', 'tensor'), may hold values from -0.125 to 0.125
- norm2_gain: float32 [2048], replicated, may hold values from 0.5 to 1.5
- w_mlp_in: float32 [2048, 2, 5632], P('dp', None, 'tensor'), may hold values from -0.125 to 0.125
- w_mlp_out: float32 [2048, 5632], P('dp', 'tensor'), may hold values from -0.078125 to 0.078125
- cotangent: bfloat16 [24576, 2048], P(('dp', 'tensor')), may hold values from -6 to 6
Outputs:
- output: bfloat16 [24576, 2048], P(('dp', 'tensor'))
- grad_inputs: float32 [24576, 2048], P(('dp', 'tensor'))
- grad_norm1_gain: float32 [2048], replicated
- grad_w_qkv: float32 [2048, 3, 2048], P('dp', None, 'tensor')
- grad_w_gate_out: float32 [2048, 2048], P('dp', 'tensor')
- grad_w_decay: float32 [2048, 2, 16], P('dp', None, 'tensor')
- grad_conv_weight: float32 [3, 4, 2048], P(None, None, 'tensor')
- grad_decay_log: float32 [16], P('tensor')
- grad_decay_bias: float32 [16], P('tensor')
- grad_head_norm_gain: float32 [128], replicated
- grad_w_output: float32 [2048, 2048], P('dp', 'tensor')
- grad_norm2_gain: float32 [2048], replicated
- grad_w_mlp_in: float32 [2048, 2, 5632], P('dp', None, 'tensor')
- grad_w_mlp_out: float32 [2048, 5632], P('dp', 'tensor')
Inputs may be any that keep to these rules, and one draw needn't show every extreme that they name: `seq_offsets`: offsets and lengths are multiples of 64. In each group the used slots come first (at least one), each of 1024 tokens or more; the sequences lie in slot order without intersection, possibly with unused rows between them, and end by 3072; an unused slot has length 0 and offset 3072. In every draw some group holds one sequence that fills it completely. `seq_lengths`: see seq_offsets.
All inputs are finite; a program needn't handle non-finite values.
Results may differ from a plain program's by a relative error of at most 0.02.
The roundings to bfloat16 on the way count: a program that leaves them out, or rounds other values in their place, can miss the bound.
Values may be sent and summed in bfloat16 or wider, within the bound.
A program may use at most 640 MiB of HBM per device.

v0:
```python
from functools import partial

import jax
import jax.numpy as jnp
from jax import lax
from jax.sharding import PartitionSpec as P

HEAD_DIM = 128
BLOCK = 64


epsilon = 1e-06
top_precision = lax.Precision.HIGHEST


def segment_info(offsets, lengths, total):
    positions = jnp.arange(total, dtype=jnp.int32)[:, None]
    inside = (positions >= offsets[None, :]) & (positions < offsets[None, :] + lengths[None, :])
    live_rows = jnp.any(inside, axis=1)
    place = jnp.sum(jnp.where(inside, positions - offsets[None, :], 0), axis=1)
    taps = jnp.arange(4, dtype=jnp.int32)
    tap_mask = place[:, None] >= 3 - taps[None, :]
    starts = jnp.arange(total // BLOCK, dtype=jnp.int32) * BLOCK
    resets = jnp.any((starts[:, None] == offsets[None, :]) & (lengths[None, :] > 0), axis=1)
    return (live_rows, tap_mask, resets)


def short_conv(values, kernel, tap_mask):
    total = values.shape[0]
    padded = jnp.pad(values, ((3, 0), (0, 0), (0, 0)))
    result = jnp.zeros_like(values)
    for kernel_tap in range(4):
        term = kernel[:, kernel_tap, :][None] * padded[kernel_tap : kernel_tap + total]
        result = result + jnp.where(tap_mask[:, kernel_tap][:, None, None], term, 0.0)
    return result


def state_step(recurrent_state, block_data):
    key_solved, value_solved, key_trailing, last_total, restart = block_data
    recurrent_state = jnp.where(restart, 0.0, recurrent_state)
    newest_value = value_solved - jnp.einsum(
        "hrq,hqm->hrm", key_solved, recurrent_state, precision=top_precision
    )
    next_state = jnp.exp(last_total)[:, None, None] * recurrent_state + jnp.einsum(
        "htf,htz->hfz", key_trailing, newest_value, precision=top_precision
    )
    return (next_state, (recurrent_state, newest_value))


def mixer_local(z_qkv, z_gate, z_decay, kernel, decay_log, decay_bias, head_gain, tap_mask, resets):
    total = z_qkv.shape[0]
    heads = decay_log.shape[0]
    blocks = total // BLOCK
    mixed = jax.nn.silu(short_conv(z_qkv, kernel, tap_mask))
    query_rows = mixed[:, 0].reshape(total, heads, HEAD_DIM)
    key_matrix_rows = mixed[:, 1].reshape(total, heads, HEAD_DIM)
    values = mixed[:, 2].reshape(total, heads, HEAD_DIM)
    query_rows = (
        query_rows
        * lax.rsqrt(jnp.sum(query_rows * query_rows, axis=-1, keepdims=True) + epsilon)
        * HEAD_DIM ** (-0.5)
    )
    key_matrix_rows = key_matrix_rows * lax.rsqrt(
        jnp.sum(key_matrix_rows * key_matrix_rows, axis=-1, keepdims=True) + epsilon
    )
    decays = -jnp.exp(decay_log) * jax.nn.softplus(z_decay[:, 0] + decay_bias)
    beta_gate = jax.nn.sigmoid(z_decay[:, 1])

    def to_blocks(array):
        return jnp.swapaxes(array.reshape((blocks, BLOCK) + array.shape[1:]), 1, 2)

    query_blocks = to_blocks(query_rows)
    key_blocks = to_blocks(key_matrix_rows)
    value_blocks = to_blocks(values)
    decay_blocks = to_blocks(decays)
    beta_blocks = to_blocks(beta_gate)
    width = BLOCK
    running_total = jnp.cumsum(decay_blocks, axis=2)
    strict_lower = jnp.tril(jnp.ones((width, width), dtype=bool), -1)
    lower_incl = jnp.tril(jnp.ones((width, width), dtype=bool))
    spread = running_total[:, :, :, None] - running_total[:, :, None, :]
    strict_decay = jnp.where(strict_lower, jnp.exp(jnp.where(strict_lower, spread, 0.0)), 0.0)
    incl_decay = jnp.where(lower_incl, jnp.exp(jnp.where(lower_incl, spread, 0.0)), 0.0)
    key_inner = jnp.einsum("bhik,bhjk->bhij", key_blocks, key_blocks, precision=top_precision)
    system = (
        jnp.eye(width, dtype=decays.dtype) + beta_blocks[:, :, :, None] * key_inner * strict_decay
    )
    right_side = jnp.concatenate(
        [
            key_blocks * (beta_blocks * jnp.exp(running_total))[:, :, :, None],
            value_blocks * beta_blocks[:, :, :, None],
        ],
        axis=3,
    )
    triangular_answer = jax.scipy.linalg.solve_triangular(
        system, right_side, lower=True, unit_diagonal=True
    )
    key_solved = triangular_answer[:, :, :, :HEAD_DIM]
    value_solved = triangular_answer[:, :, :, HEAD_DIM:]
    trailing_part = jnp.exp(running_total[:, :, -1:] - running_total)
    key_trailing = key_blocks * trailing_part[:, :, :, None]
    start_memory = jnp.zeros((heads, HEAD_DIM, HEAD_DIM), dtype=query_rows.dtype)
    _, (entry_states, newest_values) = lax.scan(
        jax.checkpoint(state_step),
        start_memory,
        (key_solved, value_solved, key_trailing, running_total[:, :, -1], resets),
    )
    scores = (
        jnp.einsum("bhik,bhjk->bhij", query_blocks, key_blocks, precision=top_precision)
        * incl_decay
    )
    output_rows = jnp.einsum(
        "bhrq,bhqm->bhrm",
        query_blocks * jnp.exp(running_total)[:, :, :, None],
        entry_states,
        precision=top_precision,
    )
    output_rows = output_rows + jnp.einsum(
        "bhij,bhjv->bhiv", scores, newest_values, precision=top_precision
    )
    output_rows = jnp.swapaxes(output_rows, 1, 2).reshape(total, heads, HEAD_DIM)
    normed = (
        output_rows
        * lax.rsqrt(jnp.mean(output_rows * output_rows, axis=-1, keepdims=True) + epsilon)
        * head_gain
    )
    return normed.reshape(total, heads * HEAD_DIM) * jax.nn.silu(z_gate)


def project_rows(left, weight):
    return lax.dot_general(
        left, weight, (((1,), (1,)), ((), ())), preferred_element_type=jnp.float32
    )


def mlp_back_rows(grad_z, weight):
    return jnp.einsum("csf,dsf->cd", grad_z, weight, preferred_element_type=jnp.float32)


def mixer_back_rows(grad_qkv, grad_gate, grad_decay, qkv_weight, gate_weight, decay_weight):
    total = jnp.einsum("csk,dsk->cd", grad_qkv, qkv_weight, preferred_element_type=jnp.float32)
    total = total + lax.dot_general(
        grad_gate, gate_weight, (((1,), (1,)), ((), ())), preferred_element_type=jnp.float32
    )
    return total + jnp.einsum(
        "csh,dsh->cd", grad_decay, decay_weight, preferred_element_type=jnp.float32
    )


def norm_back(grad_normed, base, inverse, gain):
    scaled = base * inverse
    gain_grad = jnp.sum(grad_normed * scaled, axis=0)
    inner = grad_normed * gain
    base_grad = inverse * (inner - scaled * jnp.mean(inner * scaled, axis=-1, keepdims=True))
    return (base_grad, gain_grad)


def per_device(
    inputs,
    seq_offsets,
    seq_lengths,
    norm1_gain,
    w_qkv,
    w_gate_out,
    w_decay,
    conv_weight,
    decay_log,
    decay_bias,
    head_norm_gain,
    w_output,
    norm2_gain,
    w_mlp_in,
    w_mlp_out,
    cotangent,
):
    qkv_full, gate_full, decay_full, out_full, mlp_in_full, mlp_out_full = (
        lax.all_gather(w_qkv.astype(jnp.bfloat16), "dp", axis=0, tiled=True),
        lax.all_gather(w_gate_out.astype(jnp.bfloat16), "dp", axis=0, tiled=True),
        lax.all_gather(w_decay.astype(jnp.bfloat16), "dp", axis=0, tiled=True),
        lax.all_gather(w_output.astype(jnp.bfloat16), "dp", axis=0, tiled=True),
        lax.all_gather(w_mlp_in.astype(jnp.bfloat16), "dp", axis=0, tiled=True),
        lax.all_gather(w_mlp_out.astype(jnp.bfloat16), "dp", axis=0, tiled=True),
    )
    stream = inputs.astype(jnp.float32)
    rows = stream.shape[0]
    scale_first = lax.rsqrt(jnp.mean(stream * stream, axis=-1, keepdims=True) + epsilon)
    normed_first = (stream * scale_first * norm1_gain).astype(jnp.bfloat16)
    first_all = lax.all_gather(normed_first, "tensor", axis=0, tiled=True)
    total = first_all.shape[0]
    live_rows, tap_mask, resets = segment_info(seq_offsets[0], seq_lengths[0], total)
    live_local = lax.dynamic_slice_in_dim(
        live_rows, lax.axis_index("tensor") * rows, rows, 0
    ).astype(jnp.float32)
    z_qkv = jnp.einsum("cd,dsk->csk", first_all, qkv_full, preferred_element_type=jnp.float32)
    z_gate = jnp.dot(first_all, gate_full, preferred_element_type=jnp.float32)
    z_decay = jnp.einsum("cd,dsh->csh", first_all, decay_full, preferred_element_type=jnp.float32)
    mixer_fn = partial(mixer_local, tap_mask=tap_mask, resets=resets)
    gated, mixer_back = jax.vjp(
        mixer_fn, z_qkv, z_gate, z_decay, conv_weight, decay_log, decay_bias, head_norm_gain
    )
    gated_low = gated.astype(jnp.bfloat16)
    mixer_out = lax.psum_scatter(
        project_rows(gated_low, out_full).astype(jnp.bfloat16),
        "tensor",
        scatter_dimension=0,
        tiled=True,
    ).astype(jnp.float32)
    middle = stream + mixer_out
    scale_second = lax.rsqrt(jnp.mean(middle * middle, axis=-1, keepdims=True) + epsilon)
    normed_second = (middle * scale_second * norm2_gain).astype(jnp.bfloat16)
    second_all = lax.all_gather(normed_second, "tensor", axis=0, tiled=True)
    z_mlp = jnp.einsum("cd,dsf->csf", second_all, mlp_in_full, preferred_element_type=jnp.float32)
    gate_part = z_mlp[:, 0]
    up_part = z_mlp[:, 1]
    sigma_gate = jax.nn.sigmoid(gate_part)
    silu_gate = gate_part * sigma_gate
    hidden_low = (silu_gate * up_part).astype(jnp.bfloat16)
    feed = lax.psum_scatter(
        project_rows(hidden_low, mlp_out_full).astype(jnp.bfloat16),
        "tensor",
        scatter_dimension=0,
        tiled=True,
    ).astype(jnp.float32)
    output = (live_local[:, None] * (middle + feed)).astype(jnp.bfloat16)
    grad_out = cotangent.astype(jnp.float32) * live_local[:, None]
    grad_feed_all = lax.all_gather(grad_out.astype(jnp.bfloat16), "tensor", axis=0, tiled=True)
    grad_hidden = jnp.dot(grad_feed_all, mlp_out_full, preferred_element_type=jnp.float32)
    mlp_out_grad_part = lax.dot_general(
        grad_feed_all, hidden_low, (((0,), (0,)), ((), ())), preferred_element_type=jnp.float32
    )
    grad_gate_part = grad_hidden * up_part * sigma_gate * (1.0 + gate_part * (1.0 - sigma_gate))
    grad_up_part = grad_hidden * silu_gate
    grad_z_mlp = jnp.stack([grad_gate_part, grad_up_part], axis=1).astype(jnp.bfloat16)
    mlp_in_grad_part = jnp.einsum(
        "cd,csf->dsf", second_all, grad_z_mlp, preferred_element_type=jnp.float32
    )
    grad_second = lax.psum_scatter(
        mlp_back_rows(grad_z_mlp, mlp_in_full).astype(jnp.bfloat16),
        "tensor",
        scatter_dimension=0,
        tiled=True,
    ).astype(jnp.float32)
    grad_middle_norm, gain_second_part = norm_back(grad_second, middle, scale_second, norm2_gain)
    grad_middle = grad_out + grad_middle_norm
    grad_mixer_all = lax.all_gather(grad_middle.astype(jnp.bfloat16), "tensor", axis=0, tiled=True)
    grad_gated = jnp.dot(grad_mixer_all, out_full, preferred_element_type=jnp.float32)
    output_grad_part = lax.dot_general(
        grad_mixer_all, gated_low, (((0,), (0,)), ((), ())), preferred_element_type=jnp.float32
    )
    grad_qkv, grad_gate, grad_decay, grad_kernel, grad_log_rate, grad_rate_bias, grad_head_gain = (
        mixer_back(grad_gated)
    )
    grad_qkv_low = grad_qkv.astype(jnp.bfloat16)
    grad_gate_low = grad_gate.astype(jnp.bfloat16)
    grad_decay_low = grad_decay.astype(jnp.bfloat16)
    qkv_grad_part = jnp.einsum(
        "cd,csk->dsk", first_all, grad_qkv_low, preferred_element_type=jnp.float32
    )
    gate_grad_part = lax.dot_general(
        first_all, grad_gate_low, (((0,), (0,)), ((), ())), preferred_element_type=jnp.float32
    )
    decay_grad_part = jnp.einsum(
        "cd,csh->dsh", first_all, grad_decay_low, preferred_element_type=jnp.float32
    )
    grad_first = lax.psum_scatter(
        mixer_back_rows(
            grad_qkv_low, grad_gate_low, grad_decay_low, qkv_full, gate_full, decay_full
        ).astype(jnp.bfloat16),
        "tensor",
        scatter_dimension=0,
        tiled=True,
    ).astype(jnp.float32)
    grad_stream_norm, gain_first_part = norm_back(grad_first, stream, scale_first, norm1_gain)
    grad_inputs = grad_middle + grad_stream_norm
    qkv_grad, gate_grad, decay_grad, output_grad, mlp_in_grad, mlp_out_grad = (
        lax.psum_scatter(
            qkv_grad_part.astype(jnp.bfloat16), "dp", scatter_dimension=0, tiled=True
        ).astype(jnp.float32),
        lax.psum_scatter(
            gate_grad_part.astype(jnp.bfloat16), "dp", scatter_dimension=0, tiled=True
        ).astype(jnp.float32),
        lax.psum_scatter(
            decay_grad_part.astype(jnp.bfloat16), "dp", scatter_dimension=0, tiled=True
        ).astype(jnp.float32),
        lax.psum_scatter(
            output_grad_part.astype(jnp.bfloat16), "dp", scatter_dimension=0, tiled=True
        ).astype(jnp.float32),
        lax.psum_scatter(
            mlp_in_grad_part.astype(jnp.bfloat16), "dp", scatter_dimension=0, tiled=True
        ).astype(jnp.float32),
        lax.psum_scatter(
            mlp_out_grad_part.astype(jnp.bfloat16), "dp", scatter_dimension=0, tiled=True
        ).astype(jnp.float32),
    )
    kernel_grad, log_rate_grad, rate_bias_grad = lax.psum(
        (grad_kernel, grad_log_rate, grad_rate_bias), "dp"
    )
    gain_first_grad, gain_second_grad, head_gain_grad = lax.psum(
        (gain_first_part, gain_second_part, grad_head_gain), ("dp", "tensor")
    )
    return (
        output,
        grad_inputs,
        gain_first_grad,
        qkv_grad,
        gate_grad,
        decay_grad,
        kernel_grad,
        log_rate_grad,
        rate_bias_grad,
        head_gain_grad,
        output_grad,
        gain_second_grad,
        mlp_in_grad,
        mlp_out_grad,
    )


def solution(mesh):
    placed = (
        P(("dp", "tensor"), None),
        P("dp", None),
        P("dp", None),
        P(),
        P("dp", None, "tensor"),
        P("dp", "tensor"),
        P("dp", None, "tensor"),
        P(None, None, "tensor"),
        P("tensor"),
        P("tensor"),
        P(),
        P("dp", "tensor"),
        P(),
        P("dp", None, "tensor"),
        P("dp", "tensor"),
        P(("dp", "tensor"), None),
    )
    return jax.shard_map(
        per_device,
        mesh=mesh,
        in_specs=placed,
        out_specs=(
            P(("dp", "tensor"), None),
            P(("dp", "tensor"), None),
            P(),
            P("dp", None, "tensor"),
            P("dp", "tensor"),
            P("dp", None, "tensor"),
            P(None, None, "tensor"),
            P("tensor"),
            P("tensor"),
            P(),
            P("dp", "tensor"),
            P(),
            P("dp", None, "tensor"),
            P("dp", "tensor"),
        ),
        check_vma=False,
    )
```

profile of v0, /device:TPU:0, one launch (start us, length us, event | category | flops | bytes accessed | tf_op | source)
XLA Modules:
  0.0 4211.1 jit_solution(5985950647851050294)
XLA Ops:
  58.9 220.4 %all-gather.10.cloned.1.call-done = bf16[3072,2048]{1,0:T(8,128)(2,1)} async-done(((bf16[768,2048]{1,0:T(8,128)(2,1)}), bf16[3072,2048]{1,0:T(8,128)(2,1)}) %all-gather.10.cloned.1.call-update) | async-done | bytes 12582928 | tf_op jit(solution)/shard_map/all_gather | solution.py:188
  305.5 43.6 %fusion.30 = (f32[3072,3,512]{2,0,1:T(8,128)}, f32[3072,3,512]{2,0,1:T(8,128)}) fusion(f32[3072,3,512]{2,0,1:T(8,128)} %fusion.46, f32[3,512]{1,0:T(4,128)S(1)} %get-tuple-element.849, pred[3072]{0:T(1024)(128)(4,1)S(1)} %get-tuple-element.727, f32[3,512]{1,0:T(4,128)S(1)} %get-tuple-element.850, pred[3072]{0:T(1024)(128)(4,1)S(1)} %get-tuple-element.728, ...), kind=kLoop, calls=%fused_computation.65 | loop fusion | flops 70778880 | bytes 56659968 | tf_op jit(solution)/shard_map/jvp(jit(silu))/mul | solution.py:54
  487.6 265.0 %custom-call.10 = f32[48,4,1,64,64]{0,3,4,2,1:T(8,128)} custom-call(f32[48,4,1,64,64]{0,4,3,2,1:T(8,128)} %get-tuple-element.828), custom_call_target="InvertDiagBlocksLowerTriangular" | custom-call | tf_op jit(solution)/shard_map/jvp(jit(_solve_triangular))/vmap(vmap())/triangular_solve | solution.py:95
  811.3 331.5 %while.41 = (s32[]{:T(128)}, f32[4,128,128]{2,1,0:T(8,128)S(1)}, f32[48,4,128,128]{3,2,1,0:T(8,128)}, f32[48,4,64,128]{3,2,1,0:T(8,128)}, f32[48,4,128,128]{3,2,...) while((s32[]{:T(128)}, f32[4,128,128]{2,1,0:T(8,128)S(1)}, ...), condition=%wide.region_8.9_spmd.clone, body=%wide.region_7.8_spmd.clone.sunk | while | flops 101220352 | bytes 2363067 | solution.py:103
  1232.4 206.8 %reduce-scatter.13.cloned.1.call-done = bf16[768,2048]{1,0:T(8,128)(2,1)} async-done(((bf16[3072,2048]{1,0:T(8,128)(2,1)}), bf16[768,2048]{1,0:T(8,128)(2,1)}) %reduce-scatter.13.cloned.1.call-update) | async-done | bytes 3145744 | tf_op jit(solution)/shard_map/reduce_scatter | solution.py:202
  1452.1 58.2 %all-gather.20.cloned.1.call-done = bf16[2048,2,1408]{2,0,1:T(8,128)(2,1)} async-done(((bf16[256,2,1408]{2,0,1:T(8,128)(2,1)}), bf16[2048,2,1408]{2,0,1:T(8,128)(2,1)}) %all-gather.20.cloned.1.call-update) | async-done | bytes 11534352 | tf_op jit(solution)/shard_map/all_gather | solution.py:181
  1510.3 219.8 %all-gather.18.cloned.1.call-done = bf16[3072,2048]{1,0:T(8,128)(2,1)} async-done(((bf16[768,2048]{1,0:T(8,128)(2,1)}), bf16[3072,2048]{1,0:T(8,128)(2,1)}) %all-gather.18.cloned.1.call-update) | async-done | bytes 12582928 | tf_op jit(solution)/shard_map/all_gather | solution.py:211
  1730.1 44.7 %fusion.38 = f32[3072,2,1408]{2,0,1:T(8,128)} fusion(bf16[2048,2,1408]{2,0,1:T(8,128)(2,1)} %all-gather.20.cloned.1.call-done, bf16[3072,2048]{1,0:T(8,128)(2,1)} %all-gather.18.cloned.1.call-done), kind=kOutput, calls=%fused_computation.87 | convolution fusion | flops 35433480192 | bytes 58720256 | tf_op jit(solution)/shard_map/cd,dsf->csf/dot_general | solution.py:212
  1774.8 219.1 %all-gather.24.cloned.1.call-done = bf16[3072,2048]{1,0:T(8,128)(2,1)} async-done(((bf16[768,2048]{1,0:T(8,128)(2,1)}), bf16[3072,2048]{1,0:T(8,128)(2,1)}) %all-gather.24.cloned.1.call-update) | async-done | bytes 12582928 | tf_op jit(solution)/shard_map/all_gather | solution.py:226
  1993.9 38.0 fusion.58
  2031.9 43.7 %bitcast_convert_fusion = bf16[3072,2048]{1,0:T(8,128)(2,1)} fusion(bf16[2048,2,1408]{2,0,1:T(8,128)(2,1)} %all-gather.20.cloned.1.call-done, bf16[3072,1,1408]{2,0,1:T(8,128)(2,1)} %get-tuple-element.804, bf16[3072,1,1408]{2,0,1:T(8,128)(2,1)} %get-tuple-element.803), kind=kOutput, calls=%fused_computation.53 | convolution fusion | flops 35448422400 | bytes 41418752 | tf_op jit(solution)/shard_map/csf,dsf->cd/dot_general | solution.py:137
  2075.7 210.1 %reduce-scatter.17.cloned.1.call-done = bf16[768,2048]{1,0:T(8,128)(2,1)} async-done(((bf16[3072,2048]{1,0:T(8,128)(2,1)}), bf16[768,2048]{1,0:T(8,128)(2,1)}) %reduce-scatter.17.cloned.1.call-update) | async-done | bytes 3145744 | tf_op jit(solution)/shard_map/reduce_scatter | solution.py:237
  2346.7 45.6 %fusion.48 = bf16[2048,2,1408]{2,0,1:T(8,128)(2,1)} fusion(bf16[3072,1,1408]{2,0,1:T(8,128)(2,1)} %get-tuple-element.804, bf16[3072,1,1408]{2,0,1:T(8,128)(2,1)} %get-tuple-element.803, bf16[3072,2048]{1,0:T(8,128)(2,1)} %all-gather.18.cloned.1.call-done), kind=kOutput, calls=%fused_computation.102 | convolution fusion | flops 35473850368 | bytes 41418752 | tf_op jit(solution)/shard_map/cd,csf->dsf/dot_general | solution.py:234
  2392.3 124.0 %all-gather.26.cloned.1.call-done = bf16[3072,2048]{1,0:T(8,128)(2,1)} async-done(((bf16[768,2048]{1,0:T(8,128)(2,1)}), bf16[3072,2048]{1,0:T(8,128)(2,1)}) %all-gather.26.cloned.1.call-update) | async-done | bytes 12582928 | tf_op jit(solution)/shard_map/all_gather | solution.py:245
  2567.7 26.7 fusion.115
  2605.4 561.6 %while.42 = (s32[]{:T(128)}, f32[4,128,128]{2,1,0:T(8,128)S(1)}, f32[48,4,64,128]{3,2,1,0:T(8,128)}, f32[48,4,64,128]{3,2,1,0:T(8,128)}, f32[48,4,64,128]{3,2,1,...) while((s32[]{:T(128)}, f32[4,128,128]{2,1,0:T(8,128)S(1)}, ...), condition=%wide.region_18.19_spmd.clone, body=%wide.region_16.18_spmd.clone.sunk | while | flops 252444672 | bytes 6685564 | solution.py:103
  3257.8 29.7 fusion.111
  3561.3 44.5 %multiply_reduce_fusion.4 = (f32[3,512]{1,0:T(4,128)}, f32[3,512]{1,0:T(4,128)}, f32[3,512]{1,0:T(4,128)}, f32[3,512]{1,0:T(4,128)}, f32[3072,3,512]{2,0,1:T(8,128)}) fusion(f32[3072,3,512]{2,0,1:T(8,128)} %fusion.46, pred[3072]{0:T(1024)(128)(4,1)S(1)} %copy-done.93, pred[3072]{0:T(1024)(128)(4,1)S(1)} %copy-done.97, pred[3072]{0:T(1024)(128)(4,1)S(1)} %copy-done.95, ...), kind=kLoop, calls=%fused_computation.63 | loop fusion | flops 108521472 | bytes 75534336 | tf_op jit(solution)/shard_map/transpose(jvp())/reduce_sum | solution.py:33
  3616.6 30.8 select_multiply_fusion.3
  3647.4 26.9 fusion.29
  3730.1 32.3 fusion.26
  3830.5 146.5 %reduce-scatter.19.cloned.1.call-done = bf16[768,2048]{1,0:T(8,128)(2,1)} async-done(((bf16[3072,2048]{1,0:T(8,128)(2,1)}), bf16[768,2048]{1,0:T(8,128)(2,1)}) %reduce-scatter.19.cloned.1.call-update) | async-done | bytes 3145744 | tf_op jit(solution)/shard_map/reduce_scatter | solution.py:265
  3980.9 50.4 %all-reduce.18 = (f32[2048]{0:T(1024)}, f32[128]{0:T(128)}, f32[2048]{0:T(1024)}) all-reduce(f32[2048]{0:T(1024)S(1)} %get-tuple-element.722, f32[128]{0:T(128)S(1)} %bitcast_reduce_fusion, f32[2048]{0:T(1024)S(1)} %copy-done.104), channel_id=1, replica_groups=mesh['dp'=8,'tensor'=4] {'dp','tensor'}, use_global_device_ids=true, to_apply=%region_33.34 | all-reduce | flops 4224 | bytes 33792 | tf_op jit(solution)/shard_map/psum | solution.py:298
  4031.3 162.2 %reduce-scatter.15.cloned.1.call-done = bf16[768,2048]{1,0:T(8,128)(2,1)} async-done(((bf16[3072,2048]{1,0:T(8,128)(2,1)}), bf16[768,2048]{1,0:T(8,128)(2,1)}) %reduce-scatter.15.cloned.1.call-update) | async-done | bytes 3145744 | tf_op jit(solution)/shard_map/reduce_scatter | solution.py:218
  (1453 shorter events, 1902.5 us)
Async XLA Ops:
  7.2 51.7 %all-gather.12.cloned.1.call-start = ((), (), s32[]{:S(2)}) async-start(), calls=%async_computation.11 | async-start | bytes 7077888 | tf_op jit(solution)/shard_map/all_gather | solution.py:177
  9.8 269.5 %all-gather.10.cloned.1.call-start = ((), (), s32[]{:S(2)}) async-start(), calls=%async_computation.10 | async-start | bytes 15728640 | tf_op jit(solution)/shard_map/all_gather | solution.py:188
  15.6 1178.6 %all-gather.14.cloned.1.call-start = ((), (), s32[]{:S(2)}) async-start(), calls=%async_computation.12 | async-start | bytes 2359296 | tf_op jit(solution)/shard_map/all_gather | solution.py:178
  17.4 1199.3 %all-gather.16.cloned.1.call-start = ((), (), s32[]{:S(2)}) async-start(), calls=%async_computation.13 | async-start | bytes 2359296 | tf_op jit(solution)/shard_map/all_gather | solution.py:180
  19.3 1419.9 %reduce-scatter.13.cloned.1.call-start = ((), (), s32[]{:S(2)}) async-start(), calls=%async_computation.14 | async-start | bytes 15728640 | tf_op jit(solution)/shard_map/reduce_scatter | solution.py:202
  31.5 443.3 %copy-start.81 = (pred[64,64]{1,0:T(8,128)(4,1)}, pred[64,64]{1,0:T(8,128)(4,1)S(1)}, u32[]{:S(2)}) copy-start(pred[64,64]{1,0:T(8,128)(4,1)S(1)} %get-tuple-element.853) | copy-start | bytes 12292
  31.5 443.3 %copy-start.83 = (pred[64,64]{1,0:T(8,128)(4,1)}, pred[64,64]{1,0:T(8,128)(4,1)S(1)}, u32[]{:S(2)}) copy-start(pred[64,64]{1,0:T(8,128)(4,1)S(1)} %get-tuple-element.854) | copy-start | bytes 12292
  423.6 728.2 %copy-start.19 = (f32[48,64,4]{1,2,0:T(4,128)}, f32[48,64,4]{1,2,0:T(4,128)S(1)}, u32[]{:S(2)}) copy-start(f32[48,64,4]{1,2,0:T(4,128)S(1)} %copy.314) | copy-start | bytes 147460
  1229.0 281.3 %all-gather.20.cloned.1.call-start = ((), (), s32[]{:S(2)}) async-start(), calls=%async_computation.16 | async-start | bytes 12976128 | tf_op jit(solution)/shard_map/all_gather | solution.py:181
  1232.3 497.8 %all-gather.18.cloned.1.call-start = ((), (), s32[]{:S(2)}) async-start(), calls=%async_computation.15 | async-start | bytes 15728640 | tf_op jit(solution)/shard_map/all_gather | solution.py:211
  1446.4 328.4 %all-gather.22.cloned.1.call-start = ((), (), s32[]{:S(2)}) async-start(), calls=%async_computation.17 | async-start | bytes 6488064 | tf_op jit(solution)/shard_map/all_gather | solution.py:182
  1448.9 545.0 %all-gather.24.cloned.1.call-start = ((), (), s32[]{:S(2)}) async-start(), calls=%async_computation.19 | async-start | bytes 15728640 | tf_op jit(solution)/shard_map/all_gather | solution.py:226
  1452.0 833.8 %reduce-scatter.17.cloned.1.call-start = ((), (), s32[]{:S(2)}) async-start(), calls=%async_computation.20 | async-start | bytes 15728640 | tf_op jit(solution)/shard_map/reduce_scatter | solution.py:237
  2075.6 440.7 %all-gather.26.cloned.1.call-start = ((), (), s32[]{:S(2)}) async-start(), calls=%async_computation.21 | async-start | bytes 15728640 | tf_op jit(solution)/shard_map/all_gather | solution.py:245
  2296.9 1491.3 %reduce-scatter.29.cloned.1.call-start = ((), (), s32[]{:S(2)}) async-start(), calls=%async_computation.27 | async-start | bytes 6488064 | tf_op jit(solution)/shard_map/reduce_scatter | solution.py:291
  2322.9 1467.7 %reduce-scatter.27.cloned.1.call-start = ((), (), s32[]{:S(2)}) async-start(), calls=%async_computation.26 | async-start | bytes 12976128 | tf_op jit(solution)/shard_map/reduce_scatter | solution.py:288
  2392.3 1430.4 %reduce-scatter.31.cloned.1.call-start = ((), (), s32[]{:S(2)}) async-start(), calls=%async_computation.28 | async-start | bytes 589824
  3425.3 399.1 %reduce-scatter.25.cloned.1.call-start = ((), (), s32[]{:S(2)}) async-start(), calls=%async_computation.25 | async-start | bytes 2359296 | tf_op jit(solution)/shard_map/reduce_scatter | solution.py:285
  3536.2 290.0 %reduce-scatter.23.cloned.1.call-start = ((), (), s32[]{:S(2)}) async-start(), calls=%async_computation.24 | async-start | bytes 2359296 | tf_op jit(solution)/shard_map/reduce_scatter | solution.py:279
  3647.4 180.6 %reduce-scatter.21.cloned.1.call-start = ((), (), s32[]{:S(2)}) async-start(), calls=%async_computation.23 | async-start | bytes 7077888 | tf_op jit(solution)/shard_map/reduce_scatter | solution.py:276
  3702.1 274.9 %reduce-scatter.19.cloned.1.call-start = ((), (), s32[]{:S(2)}) async-start(), calls=%async_computation.22 | async-start | bytes 15728640 | tf_op jit(solution)/shard_map/reduce_scatter | solution.py:265
  3762.4 431.1 %reduce-scatter.15.cloned.1.call-start = ((), (), s32[]{:S(2)}) async-start(), calls=%async_computation.18 | async-start | bytes 15728640 | tf_op jit(solution)/shard_map/reduce_scatter | solution.py:218
  3795.1 398.4 %copy-start.70 = (f32[768]{0:T(1024)S(1)}, f32[768]{0:T(1024)}, u32[]{:S(2)}) copy-start(f32[768]{0:T(1024)} %copy-done.68) | copy-start | bytes 9220
  3795.1 398.4 %copy-start.89 = (f32[768]{0:T(1024)S(1)}, f32[768]{0:T(1024)}, u32[]{:S(2)}) copy-start(f32[768]{0:T(1024)} %copy-done.87) | copy-start | bytes 9220
  (145 other events, 8399.4 us)
Sparse Core Ops, SparseCore 0:
  10.5 48.3 all-gather.11
  61.0 218.1 all-gather.9
  281.7 26.0 all-gather.13
  310.2 27.8 all-gather.15
  1229.1 210.0 reduce-scatter.12
  1441.5 68.7 all-gather.19
  1511.9 218.1 all-gather.17
  1732.5 41.5 all-gather.21
  1775.7 218.1 all-gather.23
  2075.8 210.0 reduce-scatter.16
  2297.0 219.2 all-gather.25
  2519.6 57.2 reduce-scatter.28
  2580.8 86.7 reduce-scatter.26
  3425.4 32.8 reduce-scatter.30
  3536.3 39.9 reduce-scatter.24
  3647.5 40.0 reduce-scatter.22
  3702.2 60.5 reduce-scatter.20
  3765.1 211.8 reduce-scatter.18
  3979.5 213.9 reduce-scatter.14
where the time goes:
time: 4230 us; the launch traced here: 4210 us
  waiting for transfers between devices  1590 us (38%)
  matrix products  1220 us (29%)
  other arithmetic  713 us (17%)
  local copies, waits for them, and re-layouts  576 us (14%)
  blocking collectives  87.9 us (2%)
    dot_general x192, matrix products, state_step(): jnp.einsum('hrq,hqm->hrm', key_solved, recurrent_state, precision=top_pre...  326 us
    another operation x2, other arithmetic, mixer_local(): jax.scipy.linalg.solve_triangular(system, right_side, lower=True, unit_di...  265 us
    all_gather x1, waiting for transfers between devices, per_device(): first_all = lax.all_gather(normed_first, 'tensor', axis=0, tiled=True)  220 us
    all_gather x1, waiting for transfers between devices, per_device(): second_all = lax.all_gather(normed_second, 'tensor', axis=0, tiled=True)  220 us
    all_gather x1, waiting for transfers between devices, per_device(): lax.all_gather(grad_out.astype(jnp.bfloat16), 'tensor', axis=0, tiled=True)  219 us
    dot_general x144, matrix products, state_step(): jnp.einsum('htf,htz->hfz', key_trailing, newest_value, precision=top_prec...  214 us
    reduce_scatter x1, waiting for transfers between devices, per_device(): lax.psum_scatter(mlp_back_rows(grad_z_mlp, mlp_in_full).astype(jnp.bfloat...  210 us
    reduce_scatter x1, waiting for transfers between devices, per_device(): lax.psum_scatter(project_rows(gated_low, out_full).astype(jnp.bfloat16),...  207 us
  transfers between devices with their start and end apart: 19, of which 10 were waited for; matrix products, arithmetic and copies ran while one was open for 56% of the time, Pallas kernels for 0%

commit v1 on v0

v1 whole, which is shorter than its diff:
```python
import functools

import jax
import jax.numpy as jnp
from jax import lax
from jax.experimental import pallas as pl
from jax.experimental.pallas import tpu as pltpu
from jax.sharding import PartitionSpec as P

HEAD_DIM = 128
BLOCK = 64
epsilon = 1e-06
top_precision = lax.Precision.HIGHEST

NN = ((1,), (0,))
NT = ((1,), (1,))
TN = ((0,), (0,))


def mm(a, b, dims=NN, passes=1):
    if passes == 6:
        return lax.dot_general(
            a, b, (dims, ((), ())), precision=top_precision, preferred_element_type=jnp.float32
        )
    ah, bh = a.astype(jnp.bfloat16), b.astype(jnp.bfloat16)
    dot = lambda x, y: lax.dot_general(
        x, y, (dims, ((), ())), preferred_element_type=jnp.float32
    )
    total = dot(ah, bh)
    if passes == 3:
        al = (a - ah.astype(jnp.float32)).astype(jnp.bfloat16)
        bl = (b - bh.astype(jnp.float32)).astype(jnp.bfloat16)
        total = total + (dot(al, bh) + dot(ah, bl))
    return total


PASS = dict(gram=3, inv=3, solve=3, state=3, out=3, back=3)


def sigmoid(v):
    return 1.0 / (1.0 + jnp.exp(-v))


def lane_sum(v):
    return jnp.sum(v, axis=-1, keepdims=True)


def block_flags(offsets_ref, lengths_ref, start):
    live = jnp.int32(0)
    fresh = jnp.int32(0)
    for slot in range(offsets_ref.shape[1]):
        first, size = offsets_ref[0, slot], lengths_ref[0, slot]
        live = live | ((start >= first) & (start < first + size)).astype(jnp.int32)
        fresh = fresh | ((start == first) & (size > 0)).astype(jnp.int32)
    return live, fresh


def as_scale(flag):
    return jnp.where(flag > 0, 1.0, 0.0).astype(jnp.float32)


def square_masks():
    row = lax.broadcasted_iota(jnp.int32, (BLOCK, BLOCK), 0)
    col = lax.broadcasted_iota(jnp.int32, (BLOCK, BLOCK), 1)
    return row, col


def conv_block(ext, taps, live):
    shifted = [ext[8:]] + [ext[8 - d : 8 - d + BLOCK] * live for d in (1, 2, 3)]
    total = taps[3:4] * shifted[0]
    for d in (1, 2, 3):
        total = total + taps[3 - d : 4 - d] * shifted[d]
    return total, shifted


def decay_block(zd, rate, bias, heads, lower):
    x = zd + bias
    soft = jnp.maximum(x, 0.0) + jnp.log1p(jnp.exp(-jnp.abs(x)))
    decay = rate * soft
    total = mm(lower, decay, NN, 6)
    beta = sigmoid(zd)
    return x, decay, total, beta


def inverse_unit_lower(systems, row, col):
    eye = jnp.where(row == col, 1.0, 0.0)
    out = None
    size = 1
    while size < BLOCK:
        pick = ((row ^ col) < 2 * size) & ((row & size) > 0) & ((col & size) == 0)
        level = [jnp.where(pick, a, 0.0) for a in systems]
        if out is None:
            out = [eye - l for l in level]
        else:
            inner = [mm(x, l, NN, PASS["inv"]) for x, l in zip(out, level)]
            out = [x - mm(i, x, NN, PASS["inv"]) for x, i in zip(out, inner)]
        size *= 2
    return out


def prepare(z_ext, zd, taps, rate, bias, live, heads, row, col):
    width = heads * HEAD_DIM
    lower = jnp.where(row >= col, 1.0, 0.0)
    conv, shifted = conv_block(z_ext, taps, live)
    gate = sigmoid(conv)
    mixed = conv * gate
    x, decay, total, beta = decay_block(zd, rate, bias, heads, lower)
    total_rows = total.T
    parts = []
    for h in range(heads):
        at = h * HEAD_DIM
        mq = mixed[:, at : at + HEAD_DIM]
        mk = mixed[:, width + at : width + at + HEAD_DIM]
        v = mixed[:, 2 * width + at : 2 * width + at + HEAD_DIM]
        rq = lax.rsqrt(lane_sum(mq * mq) + epsilon)
        rk = lax.rsqrt(lane_sum(mk * mk) + epsilon)
        qn = mq * rq
        k = mk * rk
        q = qn * HEAD_DIM**-0.5
        g = total[:, h : h + 1]
        g_row = total_rows[h : h + 1, :]
        g_last = total[BLOCK - 1 : BLOCK, h : h + 1]
        b = beta[:, heads + h : heads + h + 1]
        spread = jnp.exp(jnp.where(row >= col, g - g_row, -1e30))
        eg = jnp.exp(g)
        trail = jnp.exp(g_last - g)
        parts.append(
            dict(q=q, qn=qn, k=k, v=v, rq=rq, rk=rk, g=g, b=b, eg=eg, trail=trail,
                 trail_row=jnp.exp(g_last - g_row), spread=spread, keep=jnp.exp(g_last))
        )
    return conv, gate, shifted, x, decay, beta, parts


def forward_kernel(
    per_step, heads, offsets_ref, lengths_ref, z_ref, taps_ref, rate_ref, bias_ref, gain_ref,
    gated_ref, o_ref, states_ref, newest_ref, inverse_ref, state, halo,
):
    step = pl.program_id(0)
    width = heads * HEAD_DIM

    @pl.when(step == 0)
    def _():
        state[...] = jnp.zeros_like(state)
        halo[...] = jnp.zeros_like(halo)

    row, col = square_masks()
    rate, bias = -jnp.exp(rate_ref[...]), bias_ref[...]
    taps = taps_ref[...]
    prepared = []
    for n in range(per_step):
        at = n * BLOCK
        live, fresh = block_flags(offsets_ref, lengths_ref, (step * per_step + n) * BLOCK)
        before = halo[...] if n == 0 else z_ref[at - 8 : at, : 3 * width]
        before = before * as_scale(live * (1 - fresh))
        z_ext = jnp.concatenate([before, z_ref[at : at + BLOCK, : 3 * width]], axis=0)
        zd = z_ref[at : at + BLOCK, 4 * width : 4 * width + 128]
        _, _, _, _, _, _, parts = prepare(
            z_ext, zd, taps, rate, bias, as_scale(live), heads, row, col
        )
        for p in parts:
            p["gram"] = mm(jnp.concatenate([p["q"], p["k"]], axis=0), p["k"], NT, PASS["gram"])
        systems = [
            jnp.where(row > col, p["b"] * p["gram"][BLOCK:] * p["spread"], 0.0) for p in parts
        ]
        inverses = inverse_unit_lower(systems, row, col)
        for p, x in zip(parts, inverses):
            right = jnp.concatenate([p["k"] * (p["b"] * p["eg"]), p["v"] * p["b"]], axis=1)
            p["solved"] = mm(x, right, NN, PASS["solve"])
            p["scores"] = p["gram"][:BLOCK] * p["spread"]
            p["inverse"] = x
        prepared.append((at, as_scale(1 - fresh), parts))
    for n, (at, keep_flag, parts) in enumerate(prepared):
        for h, p in enumerate(parts):
            lanes = slice(h * HEAD_DIM, (h + 1) * HEAD_DIM)
            entry = state[h] * keep_flag
            states_ref[n, h] = entry
            both = mm(
                jnp.concatenate([p["solved"][:, :HEAD_DIM], p["q"] * p["eg"]], axis=0),
                entry, NN, PASS["state"],
            )
            newest = p["solved"][:, HEAD_DIM:] - both[:BLOCK]
            state[h] = p["keep"] * entry + mm(p["k"] * p["trail"], newest, TN, PASS["state"])
            o = both[BLOCK:] + mm(p["scores"], newest, NN, PASS["out"])
            newest_ref[at : at + BLOCK, lanes] = newest
            o_ref[at : at + BLOCK, lanes] = o
            inverse_ref[n, h] = p["inverse"]
            inv = lax.rsqrt(lane_sum(o * o) * (1.0 / HEAD_DIM) + epsilon)
            zg = z_ref[at : at + BLOCK, 3 * width + h * HEAD_DIM : 3 * width + (h + 1) * HEAD_DIM]
            gated = o * inv * gain_ref[...] * (zg * sigmoid(zg))
            gated_ref[at : at + BLOCK, lanes] = gated.astype(gated_ref.dtype)
    last = per_step * BLOCK
    halo[...] = z_ref[last - 8 : last, : 3 * width]


def backward_kernel(
    per_step, heads, steps, offsets_ref, lengths_ref, z_ref, before_ref, taps_ref, rate_ref,
    bias_ref, gain_ref, dgated_ref, o_ref, states_ref, newest_ref, inverse_ref,
    dz_ref, dtaps_ref, dgain_ref, drate_ref, dbias_ref, dstate, dhalo, carried,
):
    index = pl.program_id(0)
    step = steps - 1 - index
    width = heads * HEAD_DIM

    @pl.when(index == 0)
    def _():
        dstate[...] = jnp.zeros_like(dstate)
        dhalo[...] = jnp.zeros_like(dhalo)
        carried[...] = jnp.zeros_like(carried)
        dtaps_ref[...] = jnp.zeros_like(dtaps_ref)
        dgain_ref[...] = jnp.zeros_like(dgain_ref)
        drate_ref[...] = jnp.zeros_like(drate_ref)
        dbias_ref[...] = jnp.zeros_like(dbias_ref)

    row, col = square_masks()
    upper = jnp.where(row <= col, 1.0, 0.0)
    lane = lax.broadcasted_iota(jnp.int32, (BLOCK, 128), 1)
    below = lax.broadcasted_iota(jnp.int32, (BLOCK, 1), 0) == BLOCK - 1
    rate, bias = -jnp.exp(rate_ref[...]), bias_ref[...]
    taps, gain = taps_ref[...], gain_ref[...]
    fold = lambda v: jnp.sum(v.reshape(BLOCK // 8, 8, v.shape[1]), axis=0)
    for n in reversed(range(per_step)):
        at = n * BLOCK
        live, fresh = block_flags(offsets_ref, lengths_ref, (step * per_step + n) * BLOCK)
        before = before_ref[:, : 3 * width] if n == 0 else z_ref[at - 8 : at, : 3 * width]
        before = before * as_scale(live * (1 - fresh))
        z_ext = jnp.concatenate([before, z_ref[at : at + BLOCK, : 3 * width]], axis=0)
        zd = z_ref[at : at + BLOCK, 4 * width : 4 * width + 128]
        conv, gate, shifted, x, decay, beta, parts = prepare(
            z_ext, zd, taps, rate, bias, as_scale(live), heads, row, col
        )
        flow = as_scale(1 - fresh)
        dtotal = jnp.zeros((BLOCK, 128), jnp.float32)
        dbeta = jnp.zeros((BLOCK, 128), jnp.float32)
        dgain = jnp.zeros((BLOCK, HEAD_DIM), jnp.float32)
        dmixed = [[], [], []]
        dgates = []
        for h, p in enumerate(parts):
            lanes = slice(h * HEAD_DIM, (h + 1) * HEAD_DIM)
            q, k, v, b, spread = p["q"], p["k"], p["v"], p["b"], p["spread"]
            o = o_ref[at : at + BLOCK, lanes]
            newest = newest_ref[at : at + BLOCK, lanes]
            zg = z_ref[at : at + BLOCK, 3 * width + h * HEAD_DIM : 3 * width + (h + 1) * HEAD_DIM]
            dgated = dgated_ref[at : at + BLOCK, lanes].astype(jnp.float32)
            inv = lax.rsqrt(lane_sum(o * o) * (1.0 / HEAD_DIM) + epsilon)
            normed = o * inv
            sg = sigmoid(zg)
            silu = zg * sg
            dgates.append(dgated * (normed * gain) * (sg * (1.0 + zg * (1.0 - sg))))
            dy = dgated * silu
            dgain = dgain + dy * normed
            dn = dy * gain
            do = inv * (dn - normed * (lane_sum(dn * normed) * (1.0 / HEAD_DIM)))

            gram = mm(jnp.concatenate([q, k], axis=0), k, NT, PASS["gram"])
            scores = gram[:BLOCK] * spread
            beta_k = b * p["eg"]
            right = jnp.concatenate([k * beta_k, v * b], axis=1)
            inverse = inverse_ref[n, h]
            solved = mm(inverse, right, NN, PASS["solve"])
            entry = states_ref[n, h]
            ds = dstate[h]
            k_trail = k * p["trail"]
            dnew = mm(scores, do, TN, PASS["back"]) + mm(k_trail, ds, NN, PASS["back"])
            both = jnp.concatenate([do, dnew], axis=0)
            q_decay = q * p["eg"]
            sides = jnp.concatenate([q_decay, -solved[:, :HEAD_DIM]], axis=0)
            dentry = p["keep"] * ds + mm(sides, both, TN, PASS["back"])
            dstate[h] = dentry * flow
            dexit = carried[h : h + 1, :1]
            carried[h : h + 1, :] = flow * jnp.broadcast_to(
                lane_sum(jnp.sum(dentry * entry, axis=0, keepdims=True)), (1, 128)
            )
            dboth = mm(both, entry, NT, PASS["back"])
            dq_decay, dw = dboth[:BLOCK], -dboth[BLOCK:]
            dk_trail = mm(newest, ds, NT, PASS["back"])
            dscores = mm(do, newest, NT, PASS["back"])
            dright = mm(inverse, jnp.concatenate([dw, dnew], axis=1), TN, PASS["back"])
            dsystem = -mm(dright, solved, NT, PASS["back"])
            dgram = jnp.concatenate(
                [dscores * spread, jnp.where(row > col, dsystem * (b * spread), 0.0)], axis=0
            )
            straight = mm(dgram, k, NN, PASS["back"])
            across = mm(dgram, jnp.concatenate([q, k], axis=0), TN, PASS["back"])
            dq = straight[:BLOCK] + dq_decay * p["eg"]
            dk = (
                straight[BLOCK:] + across + dright[:, :HEAD_DIM] * beta_k + dk_trail * p["trail"]
            )
            dv = dright[:, HEAD_DIM:] * b
            dtot = lane_sum(do * o - dv * v) + jnp.where(below, dexit, 0.0)
            dbet = lane_sum(dright * solved) * (1.0 - b)
            dtotal = jnp.where(lane == h, dtot, dtotal)
            dbeta = jnp.where(lane == heads + h, dbet, dbeta)
            dqn = dq * HEAD_DIM**-0.5
            dmixed[0].append(p["rq"] * (dqn - p["qn"] * lane_sum(p["qn"] * dqn)))
            dmixed[1].append(p["rk"] * (dk - k * lane_sum(k * dk)))
            dmixed[2].append(dv)
        dmix = jnp.concatenate(dmixed[0] + dmixed[1] + dmixed[2], axis=1)
        dconv = dmix * (gate * (1.0 + conv * (1.0 - gate)))
        after = dhalo[...]
        ext = jnp.concatenate([dconv * as_scale(live), after], axis=0)
        dz = taps[3:4] * dconv
        for d in (1, 2, 3):
            dz = dz + taps[3 - d : 4 - d] * ext[d : d + BLOCK]
        dhalo[...] = dconv[:8] * as_scale(live * (1 - fresh))
        for d in range(4):
            dtaps_ref[3 - d] += fold(dconv * shifted[d])
        ddecay = mm(upper, dtotal, NN, 6)
        slope = ddecay * rate * sigmoid(x)
        dzd = slope + dbeta
        drate_ref[...] += fold(ddecay * decay)
        dbias_ref[...] += fold(slope)
        dgain_ref[...] += fold(dgain)
        dz_ref[at : at + BLOCK, : 3 * width] = dz.astype(dz_ref.dtype)
        for h in range(heads):
            dz_ref[
                at : at + BLOCK, 3 * width + h * HEAD_DIM : 3 * width + (h + 1) * HEAD_DIM
            ] = dgates[h].astype(dz_ref.dtype)
        dz_ref[at : at + BLOCK, 4 * width : 4 * width + 128] = dzd.astype(dz_ref.dtype)


def pad_lanes(v):
    return jnp.pad(v, (0, 128 - v.shape[0]))[None, :]


def mixer_forward(z, offsets, lengths, taps, decay_log, decay_bias, gain, per_step=2):
    rows, cols = z.shape
    heads = decay_log.shape[0]
    width = heads * HEAD_DIM
    blocks = rows // BLOCK
    steps = blocks // per_step
    tile = per_step * BLOCK
    smem = pl.BlockSpec(memory_space=pltpu.SMEM)
    whole = lambda shape: pl.BlockSpec(shape, lambda i: (0,) * len(shape))
    f32 = jnp.float32
    return pl.pallas_call(
        functools.partial(forward_kernel, per_step, heads),
        grid=(steps,),
        in_specs=[
            smem, smem,
            pl.BlockSpec((tile, cols), lambda i: (i, 0)),
            whole((4, 3 * width)), whole((1, 128)), whole((1, 128)), whole((1, HEAD_DIM)),
        ],
        out_specs=[
            pl.BlockSpec((tile, width), lambda i: (i, 0)),
            pl.BlockSpec((tile, width), lambda i: (i, 0)),
            pl.BlockSpec((per_step, heads, HEAD_DIM, HEAD_DIM), lambda i: (i, 0, 0, 0)),
            pl.BlockSpec((tile, width), lambda i: (i, 0)),
            pl.BlockSpec((per_step, heads, BLOCK, BLOCK), lambda i: (i, 0, 0, 0)),
        ],
        out_shape=[
            jax.ShapeDtypeStruct((rows, width), jnp.bfloat16),
            jax.ShapeDtypeStruct((rows, width), f32),
            jax.ShapeDtypeStruct((blocks, heads, HEAD_DIM, HEAD_DIM), f32),
            jax.ShapeDtypeStruct((rows, width), f32),
            jax.ShapeDtypeStruct((blocks, heads, BLOCK, BLOCK), f32),
        ],
        scratch_shapes=[
            pltpu.VMEM((heads, HEAD_DIM, HEAD_DIM), f32),
            pltpu.VMEM((8, 3 * width), f32),
        ],
        compiler_params=pltpu.CompilerParams(
            dimension_semantics=("arbitrary",), vmem_limit_bytes=48 * 1024 * 1024
        ),
        name="mixer_forward",
    )(offsets, lengths, z, taps, pad_lanes(decay_log), pad_lanes(decay_bias), gain[None, :])


def mixer_backward(
    z, offsets, lengths, taps, decay_log, decay_bias, gain, dgated, o, states, newest, inverses,
    per_step=2,
):
    rows, cols = z.shape
    heads = decay_log.shape[0]
    width = heads * HEAD_DIM
    blocks = rows // BLOCK
    steps = blocks // per_step
    tile = per_step * BLOCK
    smem = pl.BlockSpec(memory_space=pltpu.SMEM)
    whole = lambda shape: pl.BlockSpec(shape, lambda i: (0,) * len(shape))
    f32 = jnp.float32
    back = lambda i: (steps - 1 - i, 0)
    back4 = lambda i: (steps - 1 - i, 0, 0, 0)
    dz, dtaps, dgain, drate, dbias = pl.pallas_call(
        functools.partial(backward_kernel, per_step, heads, steps),
        grid=(steps,),
        in_specs=[
            smem, smem,
            pl.BlockSpec((tile, cols), back),
            pl.BlockSpec(
                (8, 3 * width), lambda i: (jnp.maximum((steps - 1 - i) * (tile // 8) - 1, 0), 0)
            ),
            whole((4, 3 * width)), whole((1, 128)), whole((1, 128)), whole((1, HEAD_DIM)),
            pl.BlockSpec((tile, width), back),
            pl.BlockSpec((tile, width), back),
            pl.BlockSpec((per_step, heads, HEAD_DIM, HEAD_DIM), back4),
            pl.BlockSpec((tile, width), back),
            pl.BlockSpec((per_step, heads, BLOCK, BLOCK), back4),
        ],
        out_specs=[
            pl.BlockSpec((tile, cols), back),
            whole((4, 8, 3 * width)), whole((8, HEAD_DIM)), whole((8, 128)), whole((8, 128)),
        ],
        out_shape=[
            jax.ShapeDtypeStruct((rows, cols), jnp.bfloat16),
            jax.ShapeDtypeStruct((4, 8, 3 * width), f32),
            jax.ShapeDtypeStruct((8, HEAD_DIM), f32),
            jax.ShapeDtypeStruct((8, 128), f32),
            jax.ShapeDtypeStruct((8, 128), f32),
        ],
        scratch_shapes=[
            pltpu.VMEM((heads, HEAD_DIM, HEAD_DIM), f32),
            pltpu.VMEM((8, 3 * width), f32),
            pltpu.VMEM((8, 128), f32),
        ],
        compiler_params=pltpu.CompilerParams(
            dimension_semantics=("arbitrary",), vmem_limit_bytes=48 * 1024 * 1024
        ),
        name="mixer_backward",
    )(
        offsets, lengths, z, z, taps, pad_lanes(decay_log), pad_lanes(decay_bias), gain[None, :],
        dgated, o, states, newest, inverses,
    )
    return (
        dz,
        jnp.sum(dtaps, axis=1),
        jnp.sum(dgain, axis=0),
        jnp.sum(drate, axis=0)[:heads],
        jnp.sum(dbias, axis=0)[:heads],
    )


def live_mask(offsets, lengths, total):
    positions = jnp.arange(total, dtype=jnp.int32)[:, None]
    inside = (positions >= offsets[None, :]) & (positions < offsets[None, :] + lengths[None, :])
    return jnp.any(inside, axis=1)


def project_rows(left, weight):
    return lax.dot_general(
        left, weight, (((1,), (1,)), ((), ())), preferred_element_type=jnp.float32
    )


def norm_back(grad_normed, base, inverse, gain):
    scaled = base * inverse
    gain_grad = jnp.sum(grad_normed * scaled, axis=0)
    inner = grad_normed * gain
    base_grad = inverse * (inner - scaled * jnp.mean(inner * scaled, axis=-1, keepdims=True))
    return (base_grad, gain_grad)


def gather_weight(weight):
    rows, columns = weight.shape
    shares = lax.all_gather(weight.astype(jnp.bfloat16), ("dp", "tensor"), axis=0, tiled=False)
    shares = shares.reshape(-1, lax.axis_size("tensor"), rows, columns)
    return jnp.transpose(shares, (0, 2, 1, 3)).reshape(shares.shape[0] * rows, -1)


def scatter_rows(left, right):
    part = lax.dot_general(
        left, right, (((0,), (0,)), ((), ())), preferred_element_type=jnp.float32
    )
    return lax.psum_scatter(part.astype(jnp.bfloat16), "dp", scatter_dimension=0, tiled=True)


def per_device(
    inputs,
    seq_offsets,
    seq_lengths,
    norm1_gain,
    w_qkv,
    w_gate_out,
    w_decay,
    conv_weight,
    decay_log,
    decay_bias,
    head_norm_gain,
    w_output,
    norm2_gain,
    w_mlp_in,
    w_mlp_out,
    cotangent,
):
    depth, width, heads = w_qkv.shape[0], w_qkv.shape[2], w_decay.shape[2]
    hidden_width = w_mlp_out.shape[1]
    low = jnp.bfloat16
    joined = jnp.concatenate(
        [
            w_qkv.reshape(depth, 3 * width),
            w_gate_out,
            w_decay.reshape(depth, 2 * heads),
            jnp.zeros((depth, 128 - 2 * heads), jnp.float32),
        ],
        axis=1,
    ).astype(low)
    stream = inputs.astype(jnp.float32)
    rows = stream.shape[0]
    scale_first = lax.rsqrt(jnp.mean(stream * stream, axis=-1, keepdims=True) + epsilon)
    normed_first = (stream * scale_first * norm1_gain).astype(low)
    mixer_full = lax.all_gather(joined, "dp", axis=0, tiled=True)
    first_all = lax.all_gather(normed_first, "tensor", axis=0, tiled=True)
    out_full = gather_weight(w_output)
    gate_full = gather_weight(w_mlp_in[:, 0])
    up_full = gather_weight(w_mlp_in[:, 1])
    down_full = gather_weight(w_mlp_out)
    total = first_all.shape[0]
    live_rows = live_mask(seq_offsets[0], seq_lengths[0], total)
    live_local = lax.dynamic_slice_in_dim(
        live_rows, lax.axis_index("tensor") * rows, rows, 0
    ).astype(jnp.float32)
    z = jnp.dot(first_all, mixer_full, preferred_element_type=jnp.float32)
    taps = jnp.transpose(conv_weight, (1, 0, 2)).reshape(4, 3 * width)
    gated_heads, mixed_out, states, newest, inverses = mixer_forward(
        z, seq_offsets, seq_lengths, taps, decay_log, decay_bias, head_norm_gain
    )
    gated = lax.all_to_all(gated_heads, "tensor", 0, 1, tiled=True)
    middle = stream + project_rows(gated, out_full)
    scale_second = lax.rsqrt(jnp.mean(middle * middle, axis=-1, keepdims=True) + epsilon)
    normed_second = (middle * scale_second * norm2_gain).astype(low)
    grad_out = cotangent.astype(jnp.float32) * live_local[:, None]
    grad_feed = grad_out.astype(low)
    gate_part = jnp.dot(normed_second, gate_full, preferred_element_type=jnp.float32)
    up_part = jnp.dot(normed_second, up_full, preferred_element_type=jnp.float32)
    sigma_gate = jax.nn.sigmoid(gate_part)
    silu_gate = gate_part * sigma_gate
    hidden = (silu_gate * up_part).astype(low)
    grad_hidden = jnp.dot(grad_feed, down_full, preferred_element_type=jnp.float32)
    grad_gate = (
        grad_hidden * up_part * sigma_gate * (1.0 + gate_part * (1.0 - sigma_gate))
    ).astype(low)
    grad_up = (grad_hidden * silu_gate).astype(low)
    grad_second = project_rows(grad_gate, gate_full) + project_rows(grad_up, up_full)
    grad_middle_norm, gain_second_part = norm_back(grad_second, middle, scale_second, norm2_gain)
    grad_middle = grad_out + grad_middle_norm
    grad_mixer = grad_middle.astype(low)
    grad_gated = lax.all_to_all(
        jnp.dot(grad_mixer, out_full, preferred_element_type=jnp.float32).astype(low),
        "tensor", 1, 0, tiled=True,
    )
    down_part = scatter_rows(grad_feed, hidden)
    gate_weight_part = scatter_rows(normed_second, grad_gate)
    up_weight_part = scatter_rows(normed_second, grad_up)
    out_part = scatter_rows(grad_mixer, gated)
    feed = project_rows(hidden, down_full)
    output = (live_local[:, None] * (middle + feed)).astype(low)
    grad_z, grad_taps, grad_head_gain, grad_log_rate, grad_rate_bias = mixer_backward(
        z, seq_offsets, seq_lengths, taps, decay_log, decay_bias, head_norm_gain,
        grad_gated, mixed_out, states, newest, inverses,
    )
    grad_kernel = jnp.transpose(grad_taps.reshape(4, 3, width), (1, 0, 2))
    shares = jnp.concatenate(
        [
            part.reshape(depth, -1, size)
            for part, size in (
                (gate_weight_part, hidden_width), (up_weight_part, hidden_width),
                (down_part, hidden_width), (out_part, width),
            )
        ],
        axis=2,
    )
    shares = lax.psum_scatter(shares, "tensor", scatter_dimension=1, tiled=True)
    shares = shares.reshape(depth, 3 * hidden_width + width).astype(jnp.float32)
    mlp_in_grad = shares[:, : 2 * hidden_width].reshape(depth, 2, hidden_width)
    mlp_out_grad = shares[:, 2 * hidden_width : 3 * hidden_width]
    output_grad = shares[:, 3 * hidden_width :]
    grad_first = lax.psum_scatter(
        project_rows(grad_z, mixer_full).astype(low), "tensor", scatter_dimension=0, tiled=True
    ).astype(jnp.float32)
    joined_grad = scatter_rows(first_all, grad_z).astype(jnp.float32)
    qkv_grad = joined_grad[:, : 3 * width].reshape(depth, 3, width)
    gate_grad = joined_grad[:, 3 * width : 4 * width]
    decay_grad = joined_grad[:, 4 * width : 4 * width + 2 * heads].reshape(depth, 2, heads)
    grad_stream_norm, gain_first_part = norm_back(grad_first, stream, scale_first, norm1_gain)
    grad_inputs = grad_middle + grad_stream_norm
    kernel_grad, log_rate_grad, rate_bias_grad = lax.psum(
        (grad_kernel, grad_log_rate, grad_rate_bias), "dp"
    )
    gain_first_grad, gain_second_grad, head_gain_grad = lax.psum(
        (gain_first_part, gain_second_part, grad_head_gain), ("dp", "tensor")
    )
    return (
        output,
        grad_inputs,
        gain_first_grad,
        qkv_grad,
        gate_grad,
        decay_grad,
        kernel_grad,
        log_rate_grad,
        rate_bias_grad,
        head_gain_grad,
        output_grad,
        gain_second_grad,
        mlp_in_grad,
        mlp_out_grad,
    )


def solution(mesh):
    placed = (
        P(("dp", "tensor"), None),
        P("dp", None),
        P("dp", None),
        P(),
        P("dp", None, "tensor"),
        P("dp", "tensor"),
        P("dp", None, "tensor"),
        P(None, None, "tensor"),
        P("tensor"),
        P("tensor"),
        P(),
        P("dp", "tensor"),
        P(),
        P("dp", None, "tensor"),
        P("dp", "tensor"),
        P(("dp", "tensor"), None),
    )
    return jax.shard_map(
        per_device,
        mesh=mesh,
        in_specs=placed,
        out_specs=(
            P(("dp", "tensor"), None),
            P(("dp", "tensor"), None),
            P(),
            P("dp", None, "tensor"),
            P("dp", "tensor"),
            P("dp", None, "tensor"),
            P(None, None, "tensor"),
            P("tensor"),
            P("tensor"),
            P(),
            P("dp", "tensor"),
            P(),
            P("dp", None, "tensor"),
            P("dp", "tensor"),
        ),
        check_vma=False,
    )
```

time: 4230 us -> 2060 us (0.49)
  matrix products: 1220 us -> 387 us
  waiting for transfers between devices: 1590 us -> 881 us
  other arithmetic: 713 us -> 31.4 us
  Pallas kernels: 0 us -> 356 us
  local copies, waits for them, and re-layouts: 576 us -> 235 us
  blocking collectives: 87.9 us -> 143 us
    dot_general x365 -> x10, matrix products: 1140 us -> 264 us  [the longest x5 127 us: scatter_rows(): lax.dot_general(left, right, (((0,), (0,)), ((), ())), preferred_element_...]
    all_gather x8 -> x5, waiting for transfers between devices: 647 us -> 178 us  [the longest x4 127 us: gather_weight(): lax.all_gather(weight.astype(jnp.bfloat16), ('dp', 'tensor'), axis=0, til...]
    pallas_call x0 -> x2, Pallas kernels: none -> 356 us  [the longest x1 210 us: mixer_backward(): pl.pallas_call(functools.partial(backward_kernel, per_step, heads, steps)...]
    reduce_scatter x9 -> x7, waiting for transfers between devices: 726 us -> 395 us  [the longest x1 202 us: per_device(): lax.psum_scatter(project_rows(grad_z, mixer_full).astype(low), 'tensor',...]
    another operation x55 -> x1, other arithmetic: 296 us -> 0.85 us  [the longest x2 265 us: mixer_local(): jax.scipy.linalg.solve_triangular(system, right_side, lower=True, unit_di...]
    squeeze x198 -> x0, local copies, waits for them, and re-layouts: 218 us -> none  [the longest x192 180 us: mixer_local(): lax.scan(jax.checkpoint(state_step), start_memory, (key_solved, value_sol...]
    reduce_sum x62 -> x4, other arithmetic: 158 us -> 0.12 us  [the longest x1 0.07 us: mixer_backward(): jnp.sum(dtaps, axis=1)]
    mul x11 -> x0, other arithmetic: 98 us -> none  [the longest x1 43.6 us: mixer_local(): mixed = jax.nn.silu(short_conv(z_qkv, kernel, tap_mask))]
  transfers between devices with their start and end apart: 19 -> 14, of which waited for: 10 -> 9; matrix products, arithmetic and copies ran while one was open for 56% -> 21% of each run, Pallas kernels for 0% -> 17%
where the time goes in v1:
time: 2060 us; the launch traced here: 2050 us
  waiting for transfers between devices  881 us (43%)
  matrix products  387 us (19%)
  Pallas kernels  356 us (17%)
  local copies, waits for them, and re-layouts  235 us (11%)
  blocking collectives  143 us (7%)
  other arithmetic  31.4 us (2%)
    all_gather x1, waiting for transfers between devices, per_device(): first_all = lax.all_gather(normed_first, 'tensor', axis=0, tiled=True)  220 us
    pallas_call x1, Pallas kernels, mixer_backward(): pl.pallas_call(functools.partial(backward_kernel, per_step, heads, steps)...  210 us
    reduce_scatter x1, waiting for transfers between devices, per_device(): lax.psum_scatter(project_rows(grad_z, mixer_full).astype(low), 'tensor',...  202 us
    pallas_call x1, Pallas kernels, mixer_forward(): pl.pallas_call(functools.partial(forward_kernel, per_step, heads), grid=(...  146 us
    dot_general x5, matrix products, scatter_rows(): lax.dot_general(left, right, (((0,), (0,)), ((), ())), preferred_element_...  127 us
    all_gather x4, waiting for transfers between devices, gather_weight(): lax.all_gather(weight.astype(jnp.bfloat16), ('dp', 'tensor'), axis=0, til...  127 us
    dot_general x5, matrix products, project_rows(): lax.dot_general(left, weight, (((1,), (1,)), ((), ())), preferred_element...  124 us
    reduce_scatter x1, waiting for transfers between devices, per_device(): shares = lax.psum_scatter(shares, 'tensor', scatter_dimension=1, tiled=True)  114 us
  transfers between devices with their start and end apart: 14, of which 9 were waited for; matrix products, arithmetic and copies ran while one was open for 21% of the time, Pallas kernels for 17%

profile of v1, /device:TPU:0, one launch (start us, length us, event | category | flops | bytes accessed | tf_op | source)
XLA Modules:
  0.0 2054.5 jit_solution(2381301711056820431)
XLA Ops:
  24.3 51.3 %all-gather.13.cloned.1.call-done = bf16[2048,2176]{0,1:T(8,128)(2,1)} async-done(((bf16[256,2176]{0,1:T(8,128)(2,1)}), bf16[2048,2176]{0,1:T(8,128)(2,1)}) %all-gather.13.cloned.1.call-update) | async-done | bytes 8912912 | tf_op jit(solution)/shard_map/all_gather | solution.py:500
  75.6 220.4 %all-gather.11.cloned.1.call-done = bf16[3072,2048]{1,0:T(8,128)(2,1)} async-done(((bf16[768,2048]{1,0:T(8,128)(2,1)}), bf16[3072,2048]{1,0:T(8,128)(2,1)}) %all-gather.11.cloned.1.call-update) | async-done | bytes 12582928 | tf_op jit(solution)/shard_map/all_gather | solution.py:501
  296.0 37.3 %fusion.21.z_ref.before_ref = f32[3072,2176]{1,0:T(8,128)} fusion(bf16[3072,2048]{1,0:T(8,128)(2,1)} %all-gather.11.cloned.1.call-done, bf16[2048,2176]{0,1:T(8,128)(2,1)} %all-gather.13.cloned.1.call-done), kind=kOutput, calls=%fused_computation.61 | convolution fusion | flops 27380416512 | bytes 48234496 | tf_op jit(solution)/shard_map/dot_general | solution.py:511
  333.3 146.5 %mixer_forward.1 = (bf16[3072,512]{1,0:T(8,128)(2,1)S(1)}, f32[3072,512]{1,0:T(8,128)}, f32[48,4,128,128]{3,2,1,0:T(8,128)}, f32[3072,512]{1,0:T(8,128)}, f32[48,4,64,64]{3,2,1,0:T(8,128)}) custom-call(s32[1,3]{1,0:T(1,128)S(1)} %copy-done.1, s32[1,3]{1,0:T(1,128)S(1)} %copy-done.2, f32[3072,2176]{1,0:T(8,128)} %fusion.21.z_ref.before_ref, ...), custom_call_target="tpu_custom_call" | custom-call | tf_op jit(solution)/shard_map/mixer_forward/pallas_call | solution.py:335
  513.7 86.9 %all-to-all-done = bf16[4,768,512]{1,2,0:T(8,128)(2,1)} async-done(((bf16[4,768,512]{1,2,0:T(8,128)(2,1)}), bf16[4,768,512]{1,2,0:T(8,128)(2,1)}, u32[]{:S(2)}, u32[]{:S(2)}) %all-to-all-start) | async-done | bytes 3145760 | tf_op jit(solution)/shard_map/all_to_all | solution.py:516
  614.9 32.7 %copy.61 = bf16[8,4,256,1408]{2,0,3,1:T(8,128)(2,1)} copy(bf16[8,4,256,1408]{3,2,1,0:T(8,128)(2,1)} %bitcast.121) | data formatting | bytes 46137344 | tf_op jit(solution)/shard_map/reshape | solution.py:455
  670.6 35.3 %all-gather.17.cloned.1.call-done = bf16[8192,1,1408]{2,0,1:T(8,128)(2,1)} async-done(((bf16[256,1,1408]{2,0,1:T(8,128)(2,1)}), bf16[8192,1,1408]{2,0,1:T(8,128)(2,1)}) %all-gather.17.cloned.1.call-update) | async-done | bytes 23068688 | tf_op jit(solution)/shard_map/all_gather | solution.py:454
  705.8 31.7 %copy.59 = bf16[8,256,4,1408]{1,0,3,2:T(8,128)(2,1)} copy(bf16[8,256,4,1408]{3,1,2,0:T(8,128)(2,1)} %bitcast.122) | data formatting | bytes 46137344 | tf_op jit(solution)/shard_map/transpose | solution.py:456
  760.5 91.4 %all-gather.19.cloned.1.call-done = bf16[8192,1,1408]{2,0,1:T(8,128)(2,1)} async-done(((bf16[256,1,1408]{2,0,1:T(8,128)(2,1)}), bf16[8192,1,1408]{2,0,1:T(8,128)(2,1)}) %all-gather.19.cloned.1.call-update) | async-done | bytes 23068688 | tf_op jit(solution)/shard_map/all_gather | solution.py:454
  851.9 31.6 %copy.60 = bf16[8,256,4,1408]{1,0,3,2:T(8,128)(2,1)} copy(bf16[8,256,4,1408]{3,1,2,0:T(8,128)(2,1)} %bitcast.123) | data formatting | bytes 46137344 | tf_op jit(solution)/shard_map/transpose | solution.py:456
  956.7 36.1 %multiply_convert_fusion = (bf16[768,5632]{1,0:T(8,128)(2,1)}, bf16[768,5632]{1,0:T(8,128)(2,1)}, bf16[768,5632]{1,0:T(8,128)(2,1)}) fusion(f32[768,5632]{1,0:T(8,128)} %fusion.22, f32[768,5632]{1,0:T(8,128)} %fusion.23, bf16[2048,5632]{0,1:T(8,128)(2,1)} %bitcast.119, bf16[768,2048]{1,0:T(8,128)(2,1)} %param.31, f32[768]{0:T(1024)S(1)} %copy-done.24), kind=kOutput, calls=%fused_computation.3 | convolution fusion | flops 17786339328 | bytes 86772736 | tf_op jit(solution)/shard_map/dot_general | solution.py:527
  1016.7 25.7 %multiply_reduce_fusion = (f32[2048]{0:T(1024)}, f32[768]{0:T(1024)S(1)}, f32[768,2048]{1,0:T(8,128)S(1)}) fusion(f32[768,2048]{1,0:T(8,128)S(1)} %copy-done.8, f32[768]{0:T(1024)S(1)} %copy-done.21, f32[2048]{0:T(1024)S(1)} %copy-done.23, f32[768,2048]{1,0:T(8,128)S(1)} %fusion.24, bf16[768,5632]{1,0:T(8,128)(2,1)} %get-tuple-element.86, ...), kind=kOutput, calls=%fused_computation.27 | convolution fusion | flops 17727748096 | bytes 50616320 | tf_op jit(solution)/shard_map/dot_general | solution.py:439
  1058.6 25.3 %convolution_convert_fusion = bf16[2048,5632]{1,0:T(8,128)(2,1)} fusion(bf16[768,5632]{1,0:T(8,128)(2,1)} %get-tuple-element.88, bf16[768,2048]{1,0:T(8,128)(2,1)S(1)} %copy-done.14, f32[768]{0:T(1024)S(1)} %copy-done.24), kind=kOutput, calls=%fused_computation | convolution fusion | flops 17732993024 | bytes 34868224 | tf_op jit(solution)/shard_map/dot_general | solution.py:460
  1085.8 25.6 %convolution_convert_fusion.1 = bf16[2048,5632]{1,0:T(8,128)(2,1)} fusion(bf16[768,2048]{1,0:T(8,128)(2,1)S(1)} %copy-done.13, bf16[768,5632]{1,0:T(8,128)(2,1)} %get-tuple-element.86), kind=kOutput, calls=%fused_computation.1 | convolution fusion | flops 17728274432 | bytes 34865152 | tf_op jit(solution)/shard_map/dot_general | solution.py:460
  1111.5 25.6 %convolution_convert_fusion.2 = bf16[2048,5632]{1,0:T(8,128)(2,1)} fusion(bf16[768,2048]{1,0:T(8,128)(2,1)S(1)} %copy-done.13, bf16[768,5632]{1,0:T(8,128)(2,1)} %get-tuple-element.87), kind=kOutput, calls=%fused_computation.2 | convolution fusion | flops 17728274432 | bytes 34865152 | tf_op jit(solution)/shard_map/dot_general | solution.py:460
  1150.7 74.2 %all_to_all.38 = bf16[768,4,512]{2,0,1:T(8,128)(2,1)S(1)} all-to-all(bf16[768,4,512]{2,0,1:T(8,128)(2,1)S(1)} %bitcast.128), channel_id=1, replica_groups=mesh['dp'=8,'tensor'=4] {'tensor'}, dimensions={1} | all-to-all | bytes 6291456 | tf_op jit(solution)/shard_map/all_to_all | solution.py:536
  1224.8 209.8 %mixer_backward.1 = (bf16[3072,2176]{1,0:T(8,128)(2,1)}, f32[4,8,1536]{2,1,0:T(8,128)S(1)}, f32[8,128]{1,0:T(8,128)S(1)}, f32[8,128]{1,0:T(8,128)S(1)}, f32[8,128]{1,0:T(8,128)S(1)}) custom-call(s32[1,3]{1,0:T(1,128)S(1)} %copy-done.1, s32[1,3]{1,0:T(1,128)S(1)} %copy-done.2, f32[3072,2176]{1,0:T(8,128)} %fusion.21.z_ref.before_ref, ...), custom_call_target="tpu_custom_call" | custom-call | tf_op jit(solution)/shard_map/mixer_backward/pallas_call | solution.py:383
  1434.7 39.4 %convolution_convert_fusion.3 = bf16[2048,2176]{1,0:T(8,128)(2,1)} fusion(bf16[3072,2048]{1,0:T(8,128)(2,1)} %all-gather.11.cloned.1.call-done, bf16[3072,2176]{1,0:T(8,128)(2,1)} %get-tuple-element.29), kind=kOutput, calls=%fused_computation.8 | convolution fusion | flops 27384872960 | bytes 34865152 | tf_op jit(solution)/shard_map/dot_general | solution.py:460
  1474.1 35.8 %convolution_convert_fusion.4 = bf16[3072,2048]{1,0:T(8,128)(2,1)} fusion(bf16[3072,2176]{1,0:T(8,128)(2,1)} %get-tuple-element.29, bf16[2048,2176]{0,1:T(8,128)(2,1)} %all-gather.13.cloned.1.call-done), kind=kOutput, calls=%fused_computation.9 | convolution fusion | flops 27386707968 | bytes 34865152 | tf_op jit(solution)/shard_map/dot_general | solution.py:439
  1518.3 59.8 %reduce-scatter.12.cloned.1.call-done = bf16[256,5632]{1,0:T(8,128)(2,1)} async-done(((bf16[2048,5632]{1,0:T(8,128)(2,1)}), bf16[256,5632]{1,0:T(8,128)(2,1)}) %reduce-scatter.12.cloned.1.call-update) | async-done | bytes 2883600 | tf_op jit(solution)/shard_map/reduce_scatter | solution.py:463
  1586.1 27.5 %multiply_convert_fusion.3 = bf16[768,2048]{1,0:T(8,128)(2,1)} fusion(f32[768,2048]{1,0:T(8,128)} %copy-done.7, bf16[768,5632]{1,0:T(8,128)(2,1)} %get-tuple-element.88, bf16[2048,5632]{0,1:T(8,128)(2,1)} %bitcast.120, f32[768]{0:T(1024)S(1)} %copy-done.25), kind=kOutput, calls=%fused_computation.32 | convolution fusion | flops 17721458688 | bytes 41159680 | tf_op jit(solution)/shard_map/dot_general | solution.py:439
  1668.6 202.1 %reduce-scatter.8.cloned.1.call-done = bf16[768,2048]{1,0:T(8,128)(2,1)} async-done(((bf16[3072,2048]{1,0:T(8,128)(2,1)}), bf16[768,2048]{1,0:T(8,128)(2,1)}) %reduce-scatter.8.cloned.1.call-update) | async-done | bytes 3145744 | tf_op jit(solution)/shard_map/reduce_scatter | solution.py:566
  1874.6 45.2 %all-reduce.2 = (f32[2048]{0:T(1024)}, f32[128]{0:T(128)}, f32[2048]{0:T(1024)}) all-reduce(f32[2048]{0:T(1024)S(1)} %get-tuple-element.78, f32[128]{0:T(128)S(1)} %reduce_sum.98, f32[2048]{0:T(1024)S(1)} %copy-done.26), channel_id=1, replica_groups=mesh['dp'=8,'tensor'=4] {'dp','tensor'}, use_global_device_ids=true, to_apply=%region_7.8 | all-reduce | flops 4224 | bytes 33792 | tf_op jit(solution)/shard_map/psum | solution.py:578
  1926.2 114.4 %reduce-scatter.20.cloned.1.call-done = bf16[256,1,4736]{2,0,1:T(8,128)(2,1)} async-done(((bf16[256,4,4736]{2,0,1:T(8,128)(2,1)}), bf16[256,1,4736]{2,0,1:T(8,128)(2,1)}) %reduce-scatter.20.cloned.1.call-update) | async-done | bytes 2424848 | tf_op jit(solution)/shard_map/reduce_scatter | solution.py:561
  (151 shorter events, 328.4 us)
Async XLA Ops:
  7.2 68.4 %all-gather.13.cloned.1.call-start = ((), (), s32[]{:S(2)}) async-start(), calls=%async_computation.10 | async-start | bytes 10027008 | tf_op jit(solution)/shard_map/all_gather | solution.py:500
  14.5 281.5 %all-gather.11.cloned.1.call-start = ((), (), s32[]{:S(2)}) async-start(), calls=%async_computation.9 | async-start | bytes 15728640 | tf_op jit(solution)/shard_map/all_gather | solution.py:501
  17.8 470.5 %all-gather.15.cloned.1.call-start = ((), (), s32[]{:S(2)}) async-start(), calls=%async_computation.18 | async-start | bytes 8650752 | tf_op jit(solution)/shard_map/all_gather | solution.py:454
  19.8 595.1 %all-gather.21.cloned.1.call-start = ((), (), s32[]{:S(2)}) async-start(), calls=%async_computation.21 | async-start | bytes 23789568 | tf_op jit(solution)/shard_map/all_gather | solution.py:454
  22.2 683.6 %all-gather.17.cloned.1.call-start = ((), (), s32[]{:S(2)}) async-start(), calls=%async_computation.19 | async-start | bytes 23789568 | tf_op jit(solution)/shard_map/all_gather | solution.py:454
  23.6 828.3 %all-gather.19.cloned.1.call-start = ((), (), s32[]{:S(2)}) async-start(), calls=%async_computation.20 | async-start | bytes 23789568 | tf_op jit(solution)/shard_map/all_gather | solution.py:454
  24.2 309.0 %copy-start = (f32[3,4,512]{2,1,0:T(4,128)S(1)}, f32[3,4,512]{2,1,0:T(4,128)}, u32[]{:S(2)}) copy-start(f32[3,4,512]{2,1,0:T(4,128)} %param.23) | copy-start | bytes 73732
  24.3 309.0 %copy-start.1 = (s32[1,3]{1,0:T(1,128)S(1)}, s32[1,3]{1,0:T(1,128)}, u32[]{:S(2)}) copy-start(s32[1,3]{1,0:T(1,128)} %offsets_ref.3) | copy-start | bytes 40
  24.3 309.0 %copy-start.2 = (s32[1,3]{1,0:T(1,128)S(1)}, s32[1,3]{1,0:T(1,128)}, u32[]{:S(2)}) copy-start(s32[1,3]{1,0:T(1,128)} %lengths_ref.3) | copy-start | bytes 40
  24.3 309.0 %copy-start.3 = (f32[128]{0:T(128)S(1)}, f32[128]{0:T(128)}, u32[]{:S(2)}) copy-start(f32[128]{0:T(128)} %param.26) | copy-start | bytes 1540
  482.5 118.1 %all-to-all-start = ((bf16[4,768,512]{1,2,0:T(8,128)(2,1)}), bf16[4,768,512]{1,2,0:T(8,128)(2,1)}, u32[]{:S(2)}, u32[]{:S(2)}) async-start(bf16[4,768,512]{1,2,0:T(8,128)(2,1)} %copy.56), calls=%async_computation | async-start | bytes 6291456 | tf_op jit(solution)/shard_map/all_to_all | solution.py:516
  487.2 1022.8 %reduce-scatter.18.cloned.1.call-start = ((), (), s32[]{:S(2)}) async-start(), calls=%async_computation.16 | async-start | bytes 9437184 | tf_op jit(solution)/shard_map/reduce_scatter | solution.py:463
  503.1 97.5 %copy-start.5 = (bf16[768,2048]{1,0:T(8,128)(2,1)S(1)}, bf16[768,2048]{1,0:T(8,128)(2,1)}, u32[]{:S(2)}) copy-start(bf16[768,2048]{1,0:T(8,128)(2,1)} %param.16) | copy-start | bytes 9437188
  614.8 316.9 %copy-start.12 = (bf16[768,2048]{1,0:T(8,128)(2,1)}, bf16[768,2048]{1,0:T(8,128)(2,1)S(1)}, u32[]{:S(2)}) copy-start(bf16[768,2048]{1,0:T(8,128)(2,1)S(1)} %multiply_convert_fusion.4) | copy-start | bytes 9437188
  1058.6 453.8 %reduce-scatter.16.cloned.1.call-start = ((), (), s32[]{:S(2)}) async-start(), calls=%async_computation.15 | async-start | bytes 25952256 | tf_op jit(solution)/shard_map/reduce_scatter | solution.py:463
  1084.0 430.5 %reduce-scatter.14.cloned.1.call-start = ((), (), s32[]{:S(2)}) async-start(), calls=%async_computation.14 | async-start | bytes 25952256 | tf_op jit(solution)/shard_map/reduce_scatter | solution.py:463
  1111.4 466.7 %reduce-scatter.12.cloned.1.call-start = ((), (), s32[]{:S(2)}) async-start(), calls=%async_computation.13 | async-start | bytes 25952256 | tf_op jit(solution)/shard_map/reduce_scatter | solution.py:463
  1137.1 519.4 %reduce-scatter.10.cloned.1.call-start = ((), (), s32[]{:S(2)}) async-start(), calls=%async_computation.12 | async-start | bytes 10027008 | tf_op jit(solution)/shard_map/reduce_scatter | solution.py:463
  1474.1 396.6 %reduce-scatter.8.cloned.1.call-start = ((), (), s32[]{:S(2)}) async-start(), calls=%async_computation.11 | async-start | bytes 15728640 | tf_op jit(solution)/shard_map/reduce_scatter | solution.py:566
  1510.0 530.7 %reduce-scatter.20.cloned.1.call-start = ((), (), s32[]{:S(2)}) async-start(), calls=%async_computation.17 | async-start | bytes 12124160 | tf_op jit(solution)/shard_map/reduce_scatter | solution.py:561
  1613.7 257.1 %copy-start.6 = (bf16[768,2048]{1,0:T(8,128)(2,1)S(1)}, bf16[768,2048]{1,0:T(8,128)(2,1)}, u32[]{:S(2)}) copy-start(bf16[768,2048]{1,0:T(8,128)(2,1)} %param.16) | copy-start | bytes 9437188
  1613.7 257.1 %copy-start.17 = (f32[2048]{0:T(1024)S(1)}, f32[2048]{0:T(1024)}, u32[]{:S(2)}) copy-start(f32[2048]{0:T(1024)} %param.19) | copy-start | bytes 24580
  1613.7 257.1 %copy-start.19 = (f32[768]{0:T(1024)S(1)}, f32[768]{0:T(1024)}, u32[]{:S(2)}) copy-start(f32[768]{0:T(1024)} %copy-done.18) | copy-start | bytes 9220
  1660.5 214.1 %copy-start.26 = (f32[2048]{0:T(1024)S(1)}, f32[2048]{0:T(1024)}, u32[]{:S(2)}) copy-start(f32[2048]{0:T(1024)} %get-tuple-element.76) | copy-start | bytes 24580
  (19 other events, 191.9 us)
Sparse Core Ops, SparseCore 0:
  14.6 60.9 all-gather.12
  77.8 218.1 all-gather.10
  299.5 75.4 all-gather.14
  377.7 169.7 all-gather.20
  550.8 154.9 all-gather.16
  709.1 142.7 all-gather.18
  1058.7 69.4 reduce-scatter.17
  1132.3 145.9 reduce-scatter.15
  1282.3 145.9 reduce-scatter.13
  1432.2 145.9 reduce-scatter.11
  1582.2 74.3 reduce-scatter.9
  1658.9 211.7 reduce-scatter.7
  1873.2 167.4 reduce-scatter.19

commit v2 on v1

--- a/solution.py
+++ b/solution.py
@@ -132,16 +132,17 @@
 
 
 def forward_kernel(
-    per_step, heads, offsets_ref, lengths_ref, z_ref, taps_ref, rate_ref, bias_ref, gain_ref,
+    per_step, heads, first, offsets_ref, lengths_ref, z_ref, taps_ref, rate_ref, bias_ref,
+    gain_ref, state_in, halo_in,
     gated_ref, o_ref, states_ref, newest_ref, inverse_ref, state, halo,
 ):
-    step = pl.program_id(0)
+    step = first + pl.program_id(0)
     width = heads * HEAD_DIM
 
-    @pl.when(step == 0)
+    @pl.when(pl.program_id(0) == 0)
     def _():
-        state[...] = jnp.zeros_like(state)
-        halo[...] = jnp.zeros_like(halo)
+        state[...] = state_in[...]
+        halo[...] = halo_in[...]
 
     row, col = square_masks()
     rate, bias = -jnp.exp(rate_ref[...]), bias_ref[...]
@@ -193,23 +194,19 @@
 
 
 def backward_kernel(
-    per_step, heads, steps, offsets_ref, lengths_ref, z_ref, before_ref, taps_ref, rate_ref,
-    bias_ref, gain_ref, dgated_ref, o_ref, states_ref, newest_ref, inverse_ref,
-    dz_ref, dtaps_ref, dgain_ref, drate_ref, dbias_ref, dstate, dhalo, carried,
+    per_step, heads, last, offsets_ref, lengths_ref, z_ref, before_ref, taps_ref, rate_ref,
+    bias_ref, gain_ref, dgated_ref, o_ref, states_ref, newest_ref, inverse_ref, *refs,
 ):
+    given, (dz_ref, *kept) = refs[:7], refs[7:]
+    dstate, dhalo, carried, dtaps_ref, dgain_ref, drate_ref, dbias_ref = kept
     index = pl.program_id(0)
-    step = steps - 1 - index
+    step = last - index
     width = heads * HEAD_DIM
 
     @pl.when(index == 0)
     def _():
-        dstate[...] = jnp.zeros_like(dstate)
-        dhalo[...] = jnp.zeros_like(dhalo)
-        carried[...] = jnp.zeros_like(carried)
-        dtaps_ref[...] = jnp.zeros_like(dtaps_ref)
-        dgain_ref[...] = jnp.zeros_like(dgain_ref)
-        drate_ref[...] = jnp.zeros_like(drate_ref)
-        dbias_ref[...] = jnp.zeros_like(dbias_ref)
+        for source, target in zip(given, kept):
+            target[...] = source[...]
 
     row, col = square_masks()
     upper = jnp.where(row <= col, 1.0, 0.0)
@@ -322,23 +319,45 @@
     return jnp.pad(v, (0, 128 - v.shape[0]))[None, :]
 
 
-def mixer_forward(z, offsets, lengths, taps, decay_log, decay_bias, gain, per_step=2):
+def forward_carry(heads):
+    return (
+        jnp.zeros((heads, HEAD_DIM, HEAD_DIM), jnp.float32),
+        jnp.zeros((8, 3 * heads * HEAD_DIM), jnp.float32),
+    )
+
+
+def backward_carry(heads):
+    wide = 3 * heads * HEAD_DIM
+    shapes = (
+        (heads, HEAD_DIM, HEAD_DIM), (8, wide), (8, 128),
+        (4, 8, wide), (8, HEAD_DIM), (8, 128), (8, 128),
+    )
+    return tuple(jnp.zeros(shape, jnp.float32) for shape in shapes)
+
+
+def whole_block(shape):
+    return pl.BlockSpec(shape, lambda i: (0,) * len(shape))
+
+
+def mixer_forward(z, offsets, lengths, params, carry, chunk, chunks, per_step=2):
     rows, cols = z.shape
-    heads = decay_log.shape[0]
+    heads = carry[0].shape[0]
     width = heads * HEAD_DIM
-    blocks = rows // BLOCK
+    blocks = rows // BLOCK // chunks
     steps = blocks // per_step
     tile = per_step * BLOCK
+    first = chunk * steps
     smem = pl.BlockSpec(memory_space=pltpu.SMEM)
-    whole = lambda shape: pl.BlockSpec(shape, lambda i: (0,) * len(shape))
     f32 = jnp.float32
-    return pl.pallas_call(
-        functools.partial(forward_kernel, per_step, heads),
+    out_rows = rows // chunks
+    out = pl.pallas_call(
+        functools.partial(forward_kernel, per_step, heads, first),
         grid=(steps,),
         in_specs=[
             smem, smem,
-            pl.BlockSpec((tile, cols), lambda i: (i, 0)),
-            whole((4, 3 * width)), whole((1, 128)), whole((1, 128)), whole((1, HEAD_DIM)),
+            pl.BlockSpec((tile, cols), lambda i: (first + i, 0)),
+            *[whole_block(p.shape) for p in params],
+            *[whole_block(c.shape) for c in carry],
         ],
         out_specs=[
             pl.BlockSpec((tile, width), lambda i: (i, 0)),
@@ -346,87 +365,73 @@
             pl.BlockSpec((per_step, heads, HEAD_DIM, HEAD_DIM), lambda i: (i, 0, 0, 0)),
             pl.BlockSpec((tile, width), lambda i: (i, 0)),
             pl.BlockSpec((per_step, heads, BLOCK, BLOCK), lambda i: (i, 0, 0, 0)),
+            *[whole_block(c.shape) for c in carry],
         ],
         out_shape=[
-            jax.ShapeDtypeStruct((rows, width), jnp.bfloat16),
-            jax.ShapeDtypeStruct((rows, width), f32),
+            jax.ShapeDtypeStruct((out_rows, width), jnp.bfloat16),
+            jax.ShapeDtypeStruct((out_rows, width), f32),
             jax.ShapeDtypeStruct((blocks, heads, HEAD_DIM, HEAD_DIM), f32),
-            jax.ShapeDtypeStruct((rows, width), f32),
+            jax.ShapeDtypeStruct((out_rows, width), f32),
             jax.ShapeDtypeStruct((blocks, heads, BLOCK, BLOCK), f32),
-        ],
-        scratch_shapes=[
-            pltpu.VMEM((heads, HEAD_DIM, HEAD_DIM), f32),
-            pltpu.VMEM((8, 3 * width), f32),
+            *[jax.ShapeDtypeStruct(c.shape, f32) for c in carry],
         ],
         compiler_params=pltpu.CompilerParams(
             dimension_semantics=("arbitrary",), vmem_limit_bytes=48 * 1024 * 1024
         ),
         name="mixer_forward",
-    )(offsets, lengths, z, taps, pad_lanes(decay_log), pad_lanes(decay_bias), gain[None, :])
+    )(offsets, lengths, z, *params, *carry)
+    return out[:5], out[5:]
 
 
 def mixer_backward(
-    z, offsets, lengths, taps, decay_log, decay_bias, gain, dgated, o, states, newest, inverses,
-    per_step=2,
+    z, offsets, lengths, params, dgated, saved, carry, chunk, chunks, per_step=2
 ):
     rows, cols = z.shape
-    heads = decay_log.shape[0]
+    heads = carry[0].shape[0]
     width = heads * HEAD_DIM
-    blocks = rows // BLOCK
+    blocks = rows // BLOCK // chunks
     steps = blocks // per_step
     tile = per_step * BLOCK
+    last = chunk * steps + steps - 1
     smem = pl.BlockSpec(memory_space=pltpu.SMEM)
-    whole = lambda shape: pl.BlockSpec(shape, lambda i: (0,) * len(shape))
     f32 = jnp.float32
     back = lambda i: (steps - 1 - i, 0)
     back4 = lambda i: (steps - 1 - i, 0, 0, 0)
-    dz, dtaps, dgain, drate, dbias = pl.pallas_call(
-        functools.partial(backward_kernel, per_step, heads, steps),
+    out = pl.pallas_call(
+        functools.partial(backward_kernel, per_step, heads, last),
         grid=(steps,),
         in_specs=[
             smem, smem,
-            pl.BlockSpec((tile, cols), back),
+            pl.BlockSpec((tile, cols), lambda i: (last - i, 0)),
             pl.BlockSpec(
-                (8, 3 * width), lambda i: (jnp.maximum((steps - 1 - i) * (tile // 8) - 1, 0), 0)
+                (8, 3 * width), lambda i: (jnp.maximum((last - i) * (tile // 8) - 1, 0), 0)
             ),
-            whole((4, 3 * width)), whole((1, 128)), whole((1, 128)), whole((1, HEAD_DIM)),
-            pl.BlockSpec((tile, width), back),
+            *[whole_block(p.shape) for p in params],
+            pl.BlockSpec((tile, width), lambda i: (last - i, 0)),
             pl.BlockSpec((tile, width), back),
             pl.BlockSpec((per_step, heads, HEAD_DIM, HEAD_DIM), back4),
             pl.BlockSpec((tile, width), back),
             pl.BlockSpec((per_step, heads, BLOCK, BLOCK), back4),
+            *[whole_block(c.shape) for c in carry],
         ],
         out_specs=[
             pl.BlockSpec((tile, cols), back),
-            whole((4, 8, 3 * width)), whole((8, HEAD_DIM)), whole((8, 128)), whole((8, 128)),
+            *[whole_block(c.shape) for c in carry],
         ],
         out_shape=[
-            jax.ShapeDtypeStruct((rows, cols), jnp.bfloat16),
-            jax.ShapeDtypeStruct((4, 8, 3 * width), f32),
-            jax.ShapeDtypeStruct((8, HEAD_DIM), f32),
-            jax.ShapeDtypeStruct((8, 128), f32),
-            jax.ShapeDtypeStruct((8, 128), f32),
-        ],
-        scratch_shapes=[
-            pltpu.VMEM((heads, HEAD_DIM, HEAD_DIM), f32),
-            pltpu.VMEM((8, 3 * width), f32),
-            pltpu.VMEM((8, 128), f32),
+            jax.ShapeDtypeStruct((rows // chunks, cols), jnp.bfloat16),
+            *[jax.ShapeDtypeStruct(c.shape, f32) for c in carry],
         ],
         compiler_params=pltpu.CompilerParams(
             dimension_semantics=("arbitrary",), vmem_limit_bytes=48 * 1024 * 1024
         ),
+        cost_estimate=pl.CostEstimate(
+            flops=blocks * heads * 1_000_000_000, bytes_accessed=blocks * heads * 400_000,
+            transcendentals=0,
+        ),
         name="mixer_backward",
-    )(
-        offsets, lengths, z, z, taps, pad_lanes(decay_log), pad_lanes(decay_bias), gain[None, :],
-        dgated, o, states, newest, inverses,
-    )
-    return (
-        dz,
-        jnp.sum(dtaps, axis=1),
-        jnp.sum(dgain, axis=0),
-        jnp.sum(drate, axis=0)[:heads],
-        jnp.sum(dbias, axis=0)[:heads],
-    )
+    )(offsets, lengths, z, z, *params, dgated, *saved, *carry)
+    return out[0], tuple(out[1:])
 
 
 def live_mask(offsets, lengths, total):
@@ -449,18 +454,135 @@
     return (base_grad, gain_grad)
 
 
-def gather_weight(weight):
-    rows, columns = weight.shape
-    shares = lax.all_gather(weight.astype(jnp.bfloat16), ("dp", "tensor"), axis=0, tiled=False)
-    shares = shares.reshape(-1, lax.axis_size("tensor"), rows, columns)
-    return jnp.transpose(shares, (0, 2, 1, 3)).reshape(shares.shape[0] * rows, -1)
-
-
-def scatter_rows(left, right):
-    part = lax.dot_general(
+def swap_cores(value):
+    size = lax.axis_size("dp")
+    return lax.ppermute(value, "dp", [(i, i ^ 1) for i in range(size)])
+
+
+def chip_groups():
+    size = lax.axis_size("dp")
+    return [list(range(core, size, 2)) for core in range(2)]
+
+
+def shift_tensor(value, distance):
+    size = lax.axis_size("tensor")
+    return lax.ppermute(value, "tensor", [(i, (i + distance) % size) for i in range(size)])
+
+
+def ring_gather(value):
+    size, me = lax.axis_size("tensor"), lax.axis_index("tensor")
+    shards = [(me, value)]
+    for step in range(1, size):
+        value = shift_tensor(value, 1)
+        shards.append(((me + size - step) % size, value))
+    return shards
+
+
+def place(shards, out=None):
+    if out is None:
+        out = jnp.zeros((len(shards),) + shards[0][1].shape, shards[0][1].dtype)
+    for owner, shard in shards:
+        out = lax.dynamic_update_index_in_dim(out, shard, owner, 0)
+    return out
+
+
+def by_core(mine, other):
+    first = lax.axis_index("dp") % 2 == 0
+    return jnp.stack([jnp.where(first, mine, other), jnp.where(first, other, mine)])
+
+
+def halves(whole):
+    core, size = lax.axis_index("dp") % 2, whole.shape[0] // 2
+    return (
+        lax.dynamic_slice_in_dim(whole, core * size, size, 0),
+        lax.dynamic_slice_in_dim(whole, (1 - core) * size, size, 0),
+    )
+
+
+def core_half_slots(shares):
+    mine, other = halves(shares)
+    slots = jnp.transpose(by_core(mine, swap_cores(other)), (0, 2, 1, 3))
+    return slots.reshape(2 * slots.shape[1], -1)
+
+
+def gather_chips(slots):
+    return lax.all_gather(slots, "dp", axis=0, tiled=True, axis_index_groups=chip_groups())
+
+
+def after(values, *events):
+    tied = lax.optimization_barrier((values, events))
+    return tied[0]
+
+
+def sum_shares(shares):
+    total = lax.psum_scatter(shares, "tensor", scatter_dimension=0, tiled=True)
+    return total[0].astype(jnp.float32)
+
+
+def scatter_chips(part):
+    return lax.psum_scatter(
+        part, "dp", scatter_dimension=0, tiled=True, axis_index_groups=chip_groups()
+    )
+
+
+def core_half_grad(part, columns):
+    keep, send = halves(part)
+    both = by_core(keep, swap_cores(send))
+    both = jnp.transpose(both.reshape(2, keep.shape[0], -1, columns), (0, 2, 1, 3))
+    return both.reshape(-1, keep.shape[0], columns)
+
+
+def outer(left, right):
+    return lax.dot_general(
         left, right, (((0,), (0,)), ((), ())), preferred_element_type=jnp.float32
-    )
-    return lax.psum_scatter(part.astype(jnp.bfloat16), "dp", scatter_dimension=0, tiled=True)
+    ).astype(jnp.bfloat16)
+
+
+def to_rows(heads_part):
+    size, me = lax.axis_size("tensor"), lax.axis_index("tensor")
+    rows, width = heads_part.shape[0] // size, heads_part.shape[1]
+    out = jnp.zeros((rows, size * width), heads_part.dtype)
+    for distance in range(size):
+        to, source = (me + distance) % size, (me + size - distance) % size
+        piece = lax.dynamic_slice_in_dim(heads_part, to * rows, rows, 0)
+        if distance:
+            piece = shift_tensor(piece, distance)
+        out = lax.dynamic_update_slice_in_dim(out, piece, source * width, 1)
+    return out
+
+
+def to_heads(rows_part):
+    size, me = lax.axis_size("tensor"), lax.axis_index("tensor")
+    rows, width = rows_part.shape[0], rows_part.shape[1] // size
+    out = jnp.zeros((size * rows, width), rows_part.dtype)
+    for distance in range(size):
+        to, source = (me + distance) % size, (me + size - distance) % size
+        piece = lax.dynamic_slice_in_dim(rows_part, to * width, width, 1)
+        if distance:
+            piece = shift_tensor(piece, distance)
+        out = lax.dynamic_update_slice_in_dim(out, piece, source * rows, 0)
+    return out
+
+
+def ring_sum(terms):
+    size, me = lax.axis_size("tensor"), lax.axis_index("tensor")
+    total = None
+    for step in range(1, size + 1):
+        own = lax.dynamic_index_in_dim(terms, (me + size - step) % size, 0, keepdims=False)
+        own = own.astype(jnp.float32)
+        total = own if total is None else own + total.astype(jnp.float32)
+        if step < size:
+            total = shift_tensor(total.astype(jnp.bfloat16), 1)
+    return total
+
+
+def sum_all(value, axes):
+    for axis in axes:
+        size, reach = lax.axis_size(axis), 1
+        while reach < size:
+            value = value + lax.ppermute(value, axis, [(i, i ^ reach) for i in range(size)])
+            reach *= 2
+    return value
 
 
 def per_device(
@@ -498,86 +620,161 @@
     scale_first = lax.rsqrt(jnp.mean(stream * stream, axis=-1, keepdims=True) + epsilon)
     normed_first = (stream * scale_first * norm1_gain).astype(low)
     mixer_full = lax.all_gather(joined, "dp", axis=0, tiled=True)
-    first_all = lax.all_gather(normed_first, "tensor", axis=0, tiled=True)
-    out_full = gather_weight(w_output)
-    gate_full = gather_weight(w_mlp_in[:, 0])
-    up_full = gather_weight(w_mlp_in[:, 1])
-    down_full = gather_weight(w_mlp_out)
-    total = first_all.shape[0]
-    live_rows = live_mask(seq_offsets[0], seq_lengths[0], total)
-    live_local = lax.dynamic_slice_in_dim(
-        live_rows, lax.axis_index("tensor") * rows, rows, 0
-    ).astype(jnp.float32)
-    z = jnp.dot(first_all, mixer_full, preferred_element_type=jnp.float32)
+    early = jnp.concatenate([w_mlp_in[:, 0], w_mlp_in[:, 1], w_output], axis=1).astype(low)
+    late = w_mlp_out.astype(low)
+    chunks = lax.axis_size("tensor")
+    early_shares = place(ring_gather(early))
+    z_room = jnp.zeros((chunks, rows, joined.shape[1]), jnp.float32)
+    first_room = jnp.zeros((chunks,) + normed_first.shape, low)
+    early_shares, z_room, first_room = lax.optimization_barrier((early_shares, z_room, first_room))
+    me = lax.axis_index("tensor")
+    gate_slots = core_half_slots(early_shares[:, :, :hidden_width])
+    up_slots = core_half_slots(early_shares[:, :, hidden_width : 2 * hidden_width])
+    out_slots = jnp.transpose(early_shares[:, :, 2 * hidden_width :], (1, 0, 2))
+    out_slots = out_slots.reshape(depth, -1)
+    moved = after(normed_first, early_shares)
+    first_shards = [(me, moved)]
+    for step in range(1, chunks):
+        moved = shift_tensor(moved, 1)
+        if step == 1:
+            moved, gate_slots, up_slots, out_slots = lax.optimization_barrier(
+                (moved, gate_slots, up_slots, out_slots)
+            )
+            out_full = lax.all_gather(out_slots, "dp", axis=0, tiled=True)
+            gate_full, up_full = gather_chips(gate_slots), gather_chips(up_slots)
+        if step == chunks - 1:
+            moved, out_full = lax.optimization_barrier((moved, out_full))
+        first_shards.append(((me + chunks - step) % chunks, moved))
+    late_shards = [(me, after(late, moved))]
+    first_all = place(first_shards, first_room).reshape(-1, stream.shape[1])
+    z = place(
+        [
+            (owner, jnp.dot(shard, mixer_full, preferred_element_type=jnp.float32))
+            for owner, shard in first_shards
+        ],
+        z_room,
+    ).reshape(first_all.shape[0], -1)
+    live_rows = live_mask(seq_offsets[0], seq_lengths[0], first_all.shape[0])
+    live_local = lax.dynamic_slice_in_dim(live_rows, me * rows, rows, 0).astype(jnp.float32)
     taps = jnp.transpose(conv_weight, (1, 0, 2)).reshape(4, 3 * width)
-    gated_heads, mixed_out, states, newest, inverses = mixer_forward(
-        z, seq_offsets, seq_lengths, taps, decay_log, decay_bias, head_norm_gain
-    )
-    gated = lax.all_to_all(gated_heads, "tensor", 0, 1, tiled=True)
+    params = (taps, pad_lanes(decay_log), pad_lanes(decay_bias), head_norm_gain[None, :])
+    carry, saved, gated_parts = forward_carry(heads), [], []
+    for chunk in range(chunks):
+        (gated_part, *kept), carry = mixer_forward(
+            z, seq_offsets, seq_lengths, params, carry, chunk, chunks
+        )
+        gated_parts.append(gated_part)
+        saved.append(kept)
+        if chunk < chunks - 1:
+            moved = shift_tensor(late_shards[-1][1], 1)
+            carry, moved = lax.optimization_barrier((carry, moved))
+            late_shards.append(((me + chunks - 1 - chunk) % chunks, moved))
+        if chunk == 0:
+            carry, gate_full = lax.optimization_barrier((carry, gate_full))
+        if chunk == chunks - 2:
+            down_slots = core_half_slots(place(late_shards))
+            carry, down_slots, up_full = lax.optimization_barrier((carry, down_slots, up_full))
+            down_full = gather_chips(down_slots)
+    gated = to_rows(jnp.concatenate(gated_parts, axis=0))
     middle = stream + project_rows(gated, out_full)
     scale_second = lax.rsqrt(jnp.mean(middle * middle, axis=-1, keepdims=True) + epsilon)
     normed_second = (middle * scale_second * norm2_gain).astype(low)
     grad_out = cotangent.astype(jnp.float32) * live_local[:, None]
     grad_feed = grad_out.astype(low)
-    gate_part = jnp.dot(normed_second, gate_full, preferred_element_type=jnp.float32)
-    up_part = jnp.dot(normed_second, up_full, preferred_element_type=jnp.float32)
+    second_pair = jnp.concatenate([normed_second, swap_cores(normed_second)], axis=0)
+    feed_grad_pair = jnp.concatenate([grad_feed, swap_cores(grad_feed)], axis=0)
+    gate_part = jnp.dot(second_pair, gate_full, preferred_element_type=jnp.float32)
+    grad_hidden = jnp.dot(feed_grad_pair, down_full, preferred_element_type=jnp.float32)
+    up_part = jnp.dot(
+        after(second_pair, grad_hidden), up_full, preferred_element_type=jnp.float32
+    )
     sigma_gate = jax.nn.sigmoid(gate_part)
     silu_gate = gate_part * sigma_gate
     hidden = (silu_gate * up_part).astype(low)
-    grad_hidden = jnp.dot(grad_feed, down_full, preferred_element_type=jnp.float32)
     grad_gate = (
         grad_hidden * up_part * sigma_gate * (1.0 + gate_part * (1.0 - sigma_gate))
     ).astype(low)
     grad_up = (grad_hidden * silu_gate).astype(low)
-    grad_second = project_rows(grad_gate, gate_full) + project_rows(grad_up, up_full)
+
+    def back_rows(at):
+        return project_rows(grad_gate[at], gate_full) + project_rows(grad_up[at], up_full)
+
+    theirs = swap_cores(back_rows(slice(rows, None)).astype(low))
+    grad_second = back_rows(slice(0, rows)) + theirs.astype(jnp.float32)
     grad_middle_norm, gain_second_part = norm_back(grad_second, middle, scale_second, norm2_gain)
     grad_middle = grad_out + grad_middle_norm
     grad_mixer = grad_middle.astype(low)
-    grad_gated = lax.all_to_all(
-        jnp.dot(grad_mixer, out_full, preferred_element_type=jnp.float32).astype(low),
-        "tensor", 1, 0, tiled=True,
-    )
-    down_part = scatter_rows(grad_feed, hidden)
-    gate_weight_part = scatter_rows(normed_second, grad_gate)
-    up_weight_part = scatter_rows(normed_second, grad_up)
-    out_part = scatter_rows(grad_mixer, gated)
-    feed = project_rows(hidden, down_full)
+    down_scattered = scatter_chips(outer(feed_grad_pair, hidden))
+    grad_gated_rows = jnp.dot(grad_mixer, out_full, preferred_element_type=jnp.float32).astype(low)
+    grad_gated = to_heads(grad_gated_rows)
+    second_pair, feed_pair = after((second_pair, hidden), grad_gated_rows)
+    gate_scattered = scatter_chips(outer(second_pair, grad_gate))
+    up_scattered = scatter_chips(outer(second_pair, grad_up))
+    carry, grad_z_parts, terms = backward_carry(heads), [], []
+    for chunk in reversed(range(chunks)):
+        grad_z_part, carry = mixer_backward(
+            z, seq_offsets, seq_lengths, params, grad_gated, saved[chunk], carry, chunk, chunks
+        )
+        grad_z_parts.insert(0, grad_z_part)
+        terms.insert(0, project_rows(grad_z_part, mixer_full).astype(low))
+        extra = ()
+        if chunk == chunks - 1:
+            extra = core_half_grad(after(down_scattered, grad_z_part), hidden_width)
+        if chunk == chunks - 2:
+            extra = core_half_grad(after(gate_scattered, grad_z_part), hidden_width)
+        if chunk == 1:
+            extra = core_half_grad(after(up_scattered, grad_z_part), hidden_width)
+        carry, terms, extra, grad_z_parts = lax.optimization_barrier(
+            (carry, terms, extra, grad_z_parts)
+        )
+        if chunk == chunks - 1:
+            down_shares = sum_shares(extra)
+        if chunk == chunks - 2:
+            gate_shares = sum_shares(extra)
+        if chunk == 1:
+            up_shares = sum_shares(extra)
+            out_part = lax.psum_scatter(
+                outer(after(grad_mixer, extra), gated), "dp", scatter_dimension=0, tiled=True
+            )
+    joined_part = outer(first_all, jnp.concatenate(grad_z_parts, axis=0))
+    down_shares, gate_shares, up_shares, out_part = after(
+        (down_shares, gate_shares, up_shares, out_part), joined_part
+    )
+    out_shares = sum_shares(jnp.transpose(out_part.reshape(depth, -1, width), (1, 0, 2)))
+    joined_grad = lax.psum_scatter(
+        joined_part, "dp", scatter_dimension=0, tiled=True
+    ).astype(jnp.float32)
+    grad_first = ring_sum(jnp.stack(terms))
+    grad_taps, grad_head_gain, grad_log_rate, grad_rate_bias = (
+        jnp.sum(value, axis=-2) for value in carry[3:]
+    )
+    mlp_out_grad, output_grad = down_shares, out_shares
+    mlp_in_grad = jnp.stack([gate_shares, up_shares], axis=1)
+    feed_pair, down_late = after((feed_pair, down_full), joined_part)
+    their_feed = swap_cores(project_rows(feed_pair[rows:], down_late).astype(low))
+    feed = project_rows(feed_pair[:rows], down_late) + their_feed.astype(jnp.float32)
     output = (live_local[:, None] * (middle + feed)).astype(low)
-    grad_z, grad_taps, grad_head_gain, grad_log_rate, grad_rate_bias = mixer_backward(
-        z, seq_offsets, seq_lengths, taps, decay_log, decay_bias, head_norm_gain,
-        grad_gated, mixed_out, states, newest, inverses,
-    )
-    grad_kernel = jnp.transpose(grad_taps.reshape(4, 3, width), (1, 0, 2))
-    shares = jnp.concatenate(
-        [
-            part.reshape(depth, -1, size)
-            for part, size in (
-                (gate_weight_part, hidden_width), (up_weight_part, hidden_width),
-                (down_part, hidden_width), (out_part, width),
-            )
-        ],
-        axis=2,
-    )
-    shares = lax.psum_scatter(shares, "tensor", scatter_dimension=1, tiled=True)
-    shares = shares.reshape(depth, 3 * hidden_width + width).astype(jnp.float32)
-    mlp_in_grad = shares[:, : 2 * hidden_width].reshape(depth, 2, hidden_width)
-    mlp_out_grad = shares[:, 2 * hidden_width : 3 * hidden_width]
-    output_grad = shares[:, 3 * hidden_width :]
-    grad_first = lax.psum_scatter(
-        project_rows(grad_z, mixer_full).astype(low), "tensor", scatter_dimension=0, tiled=True
-    ).astype(jnp.float32)
-    joined_grad = scatter_rows(first_all, grad_z).astype(jnp.float32)
     qkv_grad = joined_grad[:, : 3 * width].reshape(depth, 3, width)
     gate_grad = joined_grad[:, 3 * width : 4 * width]
     decay_grad = joined_grad[:, 4 * width : 4 * width + 2 * heads].reshape(depth, 2, heads)
     grad_stream_norm, gain_first_part = norm_back(grad_first, stream, scale_first, norm1_gain)
     grad_inputs = grad_middle + grad_stream_norm
-    kernel_grad, log_rate_grad, rate_bias_grad = lax.psum(
-        (grad_kernel, grad_log_rate, grad_rate_bias), "dp"
-    )
-    gain_first_grad, gain_second_grad, head_gain_grad = lax.psum(
-        (gain_first_part, gain_second_part, grad_head_gain), ("dp", "tensor")
-    )
+    small = jnp.concatenate(
+        [
+            gain_first_part, gain_second_part, grad_head_gain,
+            grad_taps.reshape(-1), grad_log_rate[:heads], grad_rate_bias[:heads],
+        ]
+    )
+    model, shared = gain_first_part.shape[0], 2 * gain_first_part.shape[0] + HEAD_DIM
+    small = jnp.pad(small, (0, -small.shape[0] % 1024)).reshape(-1, 128)
+    small = sum_all(small, ("dp",))
+    gains = sum_all(small[: shared // 128], ("tensor",)).reshape(-1)
+    gain_first_grad, gain_second_grad = gains[:model], gains[model : 2 * model]
+    head_gain_grad = gains[2 * model :]
+    small = small.reshape(-1)[shared:]
+    kernel_grad = jnp.transpose(small[: 12 * width].reshape(4, 3, width), (1, 0, 2))
+    log_rate_grad = small[12 * width : 12 * width + heads]
+    rate_bias_grad = small[12 * width + heads : 12 * width + 2 * heads]
     return (
         output,
         grad_inputs,

time: 2060 us -> 1620 us (0.79)
  waiting for transfers between devices: 881 us -> 488 us
  blocking collectives: 143 us -> 0 us
  local copies, waits for them, and re-layouts: 235 us -> 183 us
  starting transfers between devices: 5.61 us -> 56.6 us
  other arithmetic: 31.4 us -> 79.2 us
  matrix products: 387 us -> 423 us
    ppermute x0 -> x33, waiting for transfers between devices: none -> 487 us  [the longest x18 467 us: shift_tensor(): lax.ppermute(value, 'tensor', [(i, (i + distance) % size) for i in range(...]
    reduce_scatter x7 -> x9, waiting for transfers between devices: 395 us -> 0.05 us  [the longest x4 0.04 us: sum_shares(): total = lax.psum_scatter(shares, 'tensor', scatter_dimension=0, tiled=True)]
    all_gather x5 -> x4, waiting for transfers between devices: 347 us -> 0.01 us  [the longest x3 0.01 us: gather_chips(): lax.all_gather(slots, 'dp', axis=0, tiled=True, axis_index_groups=chip_gr...]
    all_to_all x1 -> x0, waiting for transfers between devices: 86.9 us -> none  [per_device(): gated = lax.all_to_all(gated_heads, 'tensor', 0, 1, tiled=True)]
    all_to_all x1 -> x0, blocking collectives: 74.2 us -> none  [per_device(): lax.all_to_all(jnp.dot(grad_mixer, out_full, preferred_element_type=jnp.f...]
    psum x2 -> x0, blocking collectives: 69 us -> none  [the longest x1 45.2 us: per_device(): lax.psum((gain_first_part, gain_second_part, grad_head_gain), ('dp', 'ten...]
    reshape x7 -> x4, local copies, waits for them, and re-layouts: 60.8 us -> 2.32 us  [the longest x1 2.28 us: per_device(): out_part.reshape(depth, -1, width)]
    ppermute x0 -> x33, starting transfers between devices: none -> 54.4 us  [the longest x18 48.9 us: shift_tensor(): lax.ppermute(value, 'tensor', [(i, (i + distance) % size) for i in range(...]
  transfers between devices with their start and end apart: 14 -> 47, of which waited for: 9 -> 19; matrix products, arithmetic and copies ran while one was open for 21% -> 34% of each run, Pallas kernels for 17% -> 23%
where the time goes in v2:
time: 1620 us; the launch traced here: 1610 us
  waiting for transfers between devices  488 us (30%)
  matrix products  423 us (26%)
  Pallas kernels  368 us (23%)
  local copies, waits for them, and re-layouts  183 us (11%)
  other arithmetic  79.2 us (5%)
  starting transfers between devices  56.6 us (3%)
    ppermute x18, waiting for transfers between devices, shift_tensor(): lax.ppermute(value, 'tensor', [(i, (i + distance) % size) for i in range(...  467 us
    pallas_call x4, Pallas kernels, mixer_backward(): pl.pallas_call(functools.partial(backward_kernel, per_step, heads, last),...  216 us
    dot_general x11, matrix products, project_rows(): lax.dot_general(left, weight, (((1,), (1,)), ((), ())), preferred_element...  153 us
    pallas_call x4, Pallas kernels, mixer_forward(): pl.pallas_call(functools.partial(forward_kernel, per_step, heads, first),...  152 us
    dot_general x5, matrix products, outer(): lax.dot_general(left, right, (((0,), (0,)), ((), ())), preferred_element_...  124 us
    dot_general x4, matrix products, per_device(): jnp.dot(shard, mixer_full, preferred_element_type=jnp.float32)  49.2 us
    ppermute x18, starting transfers between devices, shift_tensor(): lax.ppermute(value, 'tensor', [(i, (i + distance) % size) for i in range(...  48.9 us
    unnamed x162, local copies, waits for them, and re-layouts  46.3 us
  transfers between devices with their start and end apart: 47, of which 19 were waited for; matrix products, arithmetic and copies ran while one was open for 34% of the time, Pallas kernels for 23%

profile of v2, /device:TPU:0, one launch (start us, length us, event | category | flops | bytes accessed | tf_op | source)
XLA Modules:
  0.0 1613.9 jit_solution(17607802727839290718)
XLA Ops:
  22.3 39.3 %collective-permute-done = bf16[256,3328]{1,0:T(8,128)(2,1)} collective-permute-done((bf16[256,3328]{1,0:T(8,128)(2,1)S(1)}, bf16[256,3328]{1,0:T(8,128)(2,1)}, u32[]{:S(2)}, u32[]{:S(2)}) %collective-permute-start) | collective-permute-done | bytes 1703968 | tf_op jit(solution)/shard_map/ppermute | solution.py:469
  68.9 33.2 %collective-permute-done.1 = bf16[256,3328]{1,0:T(8,128)(2,1)} collective-permute-done((bf16[256,3328]{1,0:T(8,128)(2,1)}, bf16[256,3328]{1,0:T(8,128)(2,1)}, u32[]{:S(2)}, u32[]{:S(2)}) %collective-permute-start.1) | collective-permute-done | bytes 1703968 | tf_op jit(solution)/shard_map/ppermute | solution.py:469
  181.3 46.4 %collective-permute-done.3 = bf16[768,2048]{1,0:T(8,128)(2,1)} collective-permute-done((bf16[768,2048]{1,0:T(8,128)(2,1)}, bf16[768,2048]{1,0:T(8,128)(2,1)}, u32[]{:S(2)}, u32[]{:S(2)}) %collective-permute-start.3) | collective-permute-done | bytes 3145760 | tf_op jit(solution)/shard_map/ppermute | solution.py:469
  229.5 71.2 %collective-permute-done.6 = bf16[768,2048]{1,0:T(8,128)(2,1)} collective-permute-done((bf16[768,2048]{1,0:T(8,128)(2,1)}, bf16[768,2048]{1,0:T(8,128)(2,1)}, u32[]{:S(2)}, u32[]{:S(2)}) %collective-permute-start.6) | collective-permute-done | bytes 3145760 | tf_op jit(solution)/shard_map/ppermute | solution.py:469
  347.2 24.4 %collective-permute-done.7 = bf16[768,2048]{1,0:T(8,128)(2,1)} collective-permute-done((bf16[768,2048]{1,0:T(8,128)(2,1)}, bf16[768,2048]{1,0:T(8,128)(2,1)}, u32[]{:S(2)}, u32[]{:S(2)}) %collective-permute-start.7) | collective-permute-done | bytes 3145760 | tf_op jit(solution)/shard_map/ppermute | solution.py:469
  385.6 38.1 %mixer_forward.4 = (bf16[768,512]{1,0:T(8,128)(2,1)S(1)}, f32[768,512]{1,0:T(8,128)S(1)}, f32[12,4,128,128]{3,2,1,0:T(8,128)}, f32[768,512]{1,0:T(8,128)S(1)}, f...) custom-call(s32[1,3]{1,0:T(1,128)S(1)} %copy-done.5, s32[1,3]{1,0:T(1,128)S(1)} %copy-done.6, ...), custom_call_target="tpu_custom_call" | custom-call | tf_op jit(solution)/shard_map/mixer_forward/pallas_call | solution.py:353
  430.1 38.0 %mixer_forward.5 = (bf16[768,512]{1,0:T(8,128)(2,1)S(1)}, f32[768,512]{1,0:T(8,128)S(1)}, f32[12,4,128,128]{3,2,1,0:T(8,128)}, f32[768,512]{1,0:T(8,128)S(1)}, f...) custom-call(s32[1,3]{1,0:T(1,128)S(1)} %copy-done.5, s32[1,3]{1,0:T(1,128)S(1)} %copy-done.6, ...), custom_call_target="tpu_custom_call" | custom-call | tf_op jit(solution)/shard_map/mixer_forward/pallas_call | solution.py:353
  473.1 38.0 %mixer_forward.6 = (bf16[768,512]{1,0:T(8,128)(2,1)S(1)}, f32[768,512]{1,0:T(8,128)S(1)}, f32[12,4,128,128]{3,2,1,0:T(8,128)}, f32[768,512]{1,0:T(8,128)S(1)}, f...) custom-call(s32[1,3]{1,0:T(1,128)S(1)} %copy-done.5, s32[1,3]{1,0:T(1,128)S(1)} %copy-done.6, ...), custom_call_target="tpu_custom_call" | custom-call | tf_op jit(solution)/shard_map/mixer_forward/pallas_call | solution.py:353
  535.3 38.2 %mixer_forward.7 = (bf16[768,512]{1,0:T(8,128)(2,1)S(1)}, f32[768,512]{1,0:T(8,128)S(1)}, f32[12,4,128,128]{3,2,1,0:T(8,128)}, f32[768,512]{1,0:T(8,128)S(1)}, f...) custom-call(s32[1,3]{1,0:T(1,128)S(1)} %copy-done.5, s32[1,3]{1,0:T(1,128)S(1)} %copy-done.6, ...), custom_call_target="tpu_custom_call" | custom-call | tf_op jit(solution)/shard_map/mixer_forward/pallas_call | solution.py:353
  602.1 30.8 %collective-permute-done.13 = bf16[768,512]{1,0:T(8,128)(2,1)} collective-permute-done((bf16[768,512]{1,0:T(8,128)(2,1)}, bf16[768,512]{1,0:T(8,128)(2,1)}, u32[]{:S(2)}, u32[]{:S(2)}) %collective-permute-start.13) | collective-permute-done | bytes 786464 | tf_op jit(solution)/shard_map/ppermute | solution.py:469
  661.2 26.3 %fusion.39 = f32[1536,2816]{1,0:T(8,128)} fusion(bf16[2048,2816]{1,0:T(8,128)(2,1)} %all-gather.14.cloned.1.call-done, bf16[768,2048]{1,0:T(8,128)(2,1)} %collective-permute-done.16, bf16[768,2048]{1,0:T(8,128)(2,1)} %copy-done.50), kind=kOutput, calls=%fused_computation.67 | convolution fusion | flops 17729323008 | bytes 35127296 | tf_op jit(solution)/shard_map/dot_general | solution.py:687
  687.5 24.2 %fusion.70 = f32[1536,2816]{1,0:T(8,128)} fusion(bf16[1536,2048]{1,0:T(8,128)(2,1)S(1)} %copy-done.41, bf16[2048,2816]{1,0:T(8,128)(2,1)} %all-gather.12.cloned.1.call-done), kind=kOutput, calls=%fused_computation.183 | convolution fusion | flops 17716740096 | bytes 35127296 | tf_op jit(solution)/shard_map/dot_general | solution.py:688
  711.7 34.7 %multiply_convert_fusion.1 = (bf16[1536,2816]{1,0:T(8,128)(2,1)}, bf16[1536,2816]{1,0:T(8,128)(2,1)}, bf16[1536,2816]{1,0:T(8,128)(2,1)}) fusion(f32[1536,2816]{1,0:T(8,128)} %fusion.39, f32[1536,2816]{1,0:T(8,128)} %fusion.70, bf16[2048,2816]{1,0:T(8,128)(2,1)} %all-gather.10.cloned.1.call-done, bf16[768,2048]{1,0:T(8,128)(2,1)} %copy-done.49, ...), kind=kOutput, calls=%fused_computation.1 | convolution fusion | flops 17794203648 | bytes 78381056 | tf_op jit(solution)/shard_map/dot_general | solution.py:686
  746.4 24.4 %convolution_convert_fusion.2 = bf16[2048,2816]{1,0:T(8,128)(2,1)} fusion(bf16[1536,2816]{1,0:T(8,128)(2,1)} %get-tuple-element.282, bf16[768,2048]{1,0:T(8,128)(2,1)} %collective-permute-done.16, bf16[768,2048]{1,0:T(8,128)(2,1)} %copy-done.50), kind=kOutput, calls=%fused_computation.16 | convolution fusion | flops 17735090176 | bytes 26476544 | tf_op jit(solution)/shard_map/dot_general | solution.py:536
  879.5 24.8 %convolution_convert_fusion = bf16[2048,2816]{1,0:T(8,128)(2,1)} fusion(bf16[1536,2048]{1,0:T(8,128)(2,1)} %pad_maximum_fusion.1, bf16[1536,2816]{1,0:T(8,128)(2,1)} %get-tuple-element.349), kind=kOutput, calls=%fused_computation.14 | convolution fusion | flops 17722507264 | bytes 26476544 | tf_op jit(solution)/shard_map/dot_general | solution.py:536
  950.3 31.2 %collective-permute-done.19 = bf16[768,512]{1,0:T(8,128)(2,1)} collective-permute-done((bf16[768,512]{1,0:T(8,128)(2,1)}, bf16[768,512]{1,0:T(8,128)(2,1)}, u32[]{:S(2)}, u32[]{:S(2)}) %collective-permute-start.19) | collective-permute-done | bytes 786464 | tf_op jit(solution)/shard_map/ppermute | solution.py:469
  988.6 54.0 %mixer_backward.4 = (bf16[768,2176]{1,0:T(8,128)(2,1)}, f32[4,128,128]{2,1,0:T(8,128)S(1)}, f32[8,1536]{1,0:T(8,128)S(1)}, f32[8,128]{1,0:T(8,128)S(1)}, f32[4,8...) custom-call(s32[1,3]{1,0:T(1,128)S(1)} %copy-done.5, ...), custom_call_target="tpu_custom_call" | custom-call | flops 48000000000 | bytes 19200000 | tf_op jit(solution)/shard_map/mixer_backward/pallas_call | solution.py:400
  1062.9 54.2 %mixer_backward.5 = (bf16[768,2176]{1,0:T(8,128)(2,1)}, f32[4,128,128]{2,1,0:T(8,128)S(1)}, f32[8,1536]{1,0:T(8,128)S(1)}, f32[8,128]{1,0:T(8,128)S(1)}, f32[4,8...) custom-call(s32[1,3]{1,0:T(1,128)S(1)} %copy-done.5, ...), custom_call_target="tpu_custom_call" | custom-call | flops 48000000000 | bytes 19200000 | tf_op jit(solution)/shard_map/mixer_backward/pallas_call | solution.py:400
  1136.5 53.9 %mixer_backward.6 = (bf16[768,2176]{1,0:T(8,128)(2,1)}, f32[4,128,128]{2,1,0:T(8,128)S(1)}, f32[8,1536]{1,0:T(8,128)S(1)}, f32[8,128]{1,0:T(8,128)S(1)}, f32[4,8...) custom-call(s32[1,3]{1,0:T(1,128)S(1)} %copy-done.5, ...), custom_call_target="tpu_custom_call" | custom-call | flops 48000000000 | bytes 19200000 | tf_op jit(solution)/shard_map/mixer_backward/pallas_call | solution.py:400
  1241.3 54.0 %mixer_backward.7 = (bf16[768,2176]{1,0:T(8,128)(2,1)}, f32[4,128,128]{2,1,0:T(8,128)}, f32[8,1536]{1,0:T(8,128)}, f32[8,128]{1,0:T(8,128)}, f32[4,8,1536]{2,1,0...) custom-call(s32[1,3]{1,0:T(1,128)S(1)} %copy-done.5, s32[1,3]{1,0:T(1,128)S(1)} %copy-done.6, ...), custom_call_target="tpu_custom_call" | custom-call | flops 48000000000 | bytes 19200000 | tf_op jit(solution)/shard_map/mixer_backward/pallas_call | solution.py:400
  1332.3 39.6 %fusion.9 = bf16[2048,2176]{1,0:T(8,128)(2,1)} fusion(bf16[3072,2048]{1,0:T(8,128)(2,1)} %bitcast.223, bf16[768,2176]{1,0:T(8,128)(2,1)} %get-tuple-element.281, bf16[768,2176]{1,0:T(8,128)(2,1)} %get-tuple-element.280, bf16[768,2176]{1,0:T(8,128)(2,1)} %get-tuple-element.279, bf16[768,2176]{1,0:T(8,128)(2,1)} %get-tuple-element.278), kind=kOutput, calls=%fused_computation.17 | convolution fusion | flops 27438350336 | bytes 34865152 | tf_op jit(solution)/shard_map/dot_general | solution.py:536
  1372.1 29.9 %collective-permute-done.25 = bf16[768,2048]{1,0:T(8,128)(2,1)} collective-permute-done((bf16[768,2048]{1,0:T(8,128)(2,1)}, bf16[768,2048]{1,0:T(8,128)(2,1)}, u32[]{:S(2)}, u32[]{:S(2)}) %collective-permute-start.25) | collective-permute-done | bytes 3145760 | tf_op jit(solution)/shard_map/ppermute | solution.py:469
  1426.9 53.2 %collective-permute-done.26 = bf16[768,2048]{1,0:T(8,128)(2,1)} collective-permute-done((bf16[768,2048]{1,0:T(8,128)(2,1)}, bf16[768,2048]{1,0:T(8,128)(2,1)}, u32[]{:S(2)}, u32[]{:S(2)}) %collective-permute-start.26) | collective-permute-done | bytes 3145760 | tf_op jit(solution)/shard_map/ppermute | solution.py:469
  1505.5 51.8 %collective-permute-done.27 = bf16[768,2048]{1,0:T(8,128)(2,1)} collective-permute-done((bf16[768,2048]{1,0:T(8,128)(2,1)}, bf16[768,2048]{1,0:T(8,128)(2,1)}, u32[]{:S(2)}, u32[]{:S(2)}) %collective-permute-start.27) | collective-permute-done | bytes 3145760 | tf_op jit(solution)/shard_map/ppermute | solution.py:469
  (403 shorter events, 644.8 us)
Async XLA Ops:
  7.2 293.8 %all-gather.6.cloned.1.call-start = ((), (), s32[]{:S(2)}) async-start(), calls=%async_computation.9 | async-start | bytes 10027008 | tf_op jit(solution)/shard_map/all_gather | solution.py:622
  12.4 359.2 %all-gather.8.cloned.1.call-start = ((), (), s32[]{:S(2)}) async-start(), calls=%async_computation.10 | async-start | bytes 9437184 | tf_op jit(solution)/shard_map/all_gather | solution.py:643
  155.3 72.4 %collective-permute-start.3 = (bf16[768,2048]{1,0:T(8,128)(2,1)}, bf16[768,2048]{1,0:T(8,128)(2,1)}, u32[]{:S(2)}, u32[]{:S(2)}) collective-permute-start(bf16[768,2048]{1,0:T(8,128)(2,1)} %fusion.16), channel_id=1, source_target_pairs={{0,1},{1,2},{2,3},{3,0},{4,5},{5,6},{6,7},{7,4},{8,9},{9,10},{10,1... | collective-permute-start | bytes 9437192 | tf_op jit(solution)/shard_map/ppermute | solution.py:469
  227.7 202.3 %all-gather.10.cloned.1.call-start = ((), (), s32[]{:S(2)}) async-start(), calls=%async_computation.11 | async-start | bytes 14417920 | tf_op jit(solution)/shard_map/all_gather | solution.py:509
  228.5 306.1 %all-gather.12.cloned.1.call-start = ((), (), s32[]{:S(2)}) async-start(), calls=%async_computation.12 | async-start | bytes 14417920 | tf_op jit(solution)/shard_map/all_gather | solution.py:509
  229.0 432.1 %all-gather.14.cloned.1.call-start = ((), (), s32[]{:S(2)}) async-start(), calls=%async_computation.13 | async-start | bytes 14417920 | tf_op jit(solution)/shard_map/all_gather | solution.py:509
  229.1 71.6 %collective-permute-start.6 = (bf16[768,2048]{1,0:T(8,128)(2,1)}, bf16[768,2048]{1,0:T(8,128)(2,1)}, u32[]{:S(2)}, u32[]{:S(2)}) collective-permute-start(bf16[768,2048]{1,0:T(8,128)(2,1)} %collective-permute-done.3), channel_id=1, source_target_pairs={{0,1},{1,2},{2,3},{3,0},{4,5},{5,6},{6,7},{7,4},{8,9},{9,10},{10,1... | collective-permute-start | bytes 9437192 | tf_op jit(solution)/shard_map/ppermute | solution.py:469
  300.7 70.8 %collective-permute-start.7 = (bf16[768,2048]{1,0:T(8,128)(2,1)}, bf16[768,2048]{1,0:T(8,128)(2,1)}, u32[]{:S(2)}, u32[]{:S(2)}) collective-permute-start(bf16[768,2048]{1,0:T(8,128)(2,1)} %collective-permute-done.6), channel_id=1, source_target_pairs={{0,1},{1,2},{2,3},{3,0},{4,5},{5,6},{6,7},{7,4},{8,9},{9,10},{10,1... | collective-permute-start | bytes 9437192 | tf_op jit(solution)/shard_map/ppermute | solution.py:469
  371.6 55.6 %collective-permute-start.8 = (bf16[256,1408]{0,1:T(8,128)(2,1)S(1)}, bf16[256,1408]{0,1:T(8,128)(2,1)S(1)}, u32[]{:S(2)}, u32[]{:S(2)}) collective-permute-start(bf16[256,1408]{0,1:T(8,128)(2,1)S(1)} %copy.63), channel_id=1, source_target_pairs={{0,1},{1,2},{2,3},{3,0},{4,5},{5,6},{6,7},{7,4},{8,9},{9,10},{10,1... | collective-permute-start | bytes 2162696 | tf_op jit(solution)/shard_map/ppermute | solution.py:469
  534.6 508.1 %reduce-scatter.10.cloned.1.call-start = ((), (), s32[]{:S(2)}) async-start(), calls=%async_computation.14 | async-start | bytes 14417920 | tf_op jit(solution)/shard_map/reduce_scatter | solution.py:523
  770.8 346.3 %reduce-scatter.12.cloned.1.call-start = ((), (), s32[]{:S(2)}) async-start(), calls=%async_computation.15 | async-start | bytes 14417920 | tf_op jit(solution)/shard_map/reduce_scatter | solution.py:523
  879.5 311.0 %reduce-scatter.14.cloned.1.call-start = ((), (), s32[]{:S(2)}) async-start(), calls=%async_computation.16 | async-start | bytes 14417920 | tf_op jit(solution)/shard_map/reduce_scatter | solution.py:523
  904.3 520.3 %reduce-scatter.18.cloned.1.call-start = ((), (), s32[]{:S(2)}) async-start(), calls=%async_computation.18 | async-start | bytes 3604480 | tf_op jit(solution)/shard_map/reduce_scatter | solution.py:518
  925.7 55.8 %collective-permute-start.19 = (bf16[768,512]{1,0:T(8,128)(2,1)}, bf16[768,512]{1,0:T(8,128)(2,1)}, u32[]{:S(2)}, u32[]{:S(2)}) collective-permute-start(bf16[768,512]{1,0:T(8,128)(2,1)} %get-tuple-element.366), channel_id=1, source_target_pairs={{0,2},{1,3},{2,0},{3,1},{4,6},{5,7},{6,4},{7,5},{8,10},{9,11},{10,... | collective-permute-start | bytes 2359304 | tf_op jit(solution)/shard_map/ppermute | solution.py:469
  929.8 53.8 %collective-permute-start.20 = (bf16[768,512]{1,0:T(8,128)(2,1)S(1)}, bf16[768,512]{1,0:T(8,128)(2,1)}, u32[]{:S(2)}, u32[]{:S(2)}) collective-permute-start(bf16[768,512]{1,0:T(8,128)(2,1)S(1)} %get-tuple-element.365), channel_id=1, source_target_pairs={{0,3},{1,0},{2,1},{3,2},{4,7},{5,4},{6,5},{7,6},{8,11},{9,8},{10,9... | collective-permute-start | bytes 2359304 | tf_op jit(solution)/shard_map/ppermute | solution.py:469
  1059.6 443.5 %reduce-scatter.20.cloned.1.call-start = ((), (), s32[]{:S(2)}) async-start(), calls=%async_computation.19 | async-start | bytes 3604480 | tf_op jit(solution)/shard_map/reduce_scatter | solution.py:518
  1133.5 428.5 %reduce-scatter.22.cloned.1.call-start = ((), (), s32[]{:S(2)}) async-start(), calls=%async_computation.20 | async-start | bytes 3604480 | tf_op jit(solution)/shard_map/reduce_scatter | solution.py:518
  1207.4 362.8 %reduce-scatter.24.cloned.1.call-start = ((), (), s32[]{:S(2)}) async-start(), calls=%async_computation.21 | async-start | bytes 9437184 | tf_op jit(solution)/shard_map/reduce_scatter | solution.py:736
  1218.9 379.7 %reduce-scatter.16.cloned.1.call-start = ((), (), s32[]{:S(2)}) async-start(), calls=%async_computation.17 | async-start | bytes 10027008 | tf_op jit(solution)/shard_map/reduce_scatter | solution.py:744
  1316.0 86.1 %collective-permute-start.25 = (bf16[768,2048]{1,0:T(8,128)(2,1)}, bf16[768,2048]{1,0:T(8,128)(2,1)}, u32[]{:S(2)}, u32[]{:S(2)}) collective-permute-start(bf16[768,2048]{1,0:T(8,128)(2,1)} %dynamic-slice_bitcast_fusion), channel_id=1, source_target_pairs={{0,1},{1,2},{2,3},{3,0},{4,5},{5,6},{6,7},{7,4},{8,9},{9,10},{10,1... | collective-permute-start | bytes 9437192 | tf_op jit(solution)/shard_map/ppermute | solution.py:469
  1371.9 233.5 %reduce-scatter.26.cloned.1.call-start = ((), (), s32[]{:S(2)}) async-start(), calls=%async_computation.22 | async-start | bytes 1310720 | tf_op jit(solution)/shard_map/reduce_scatter | solution.py:518
  1408.1 72.0 %collective-permute-start.26 = (bf16[768,2048]{1,0:T(8,128)(2,1)}, bf16[768,2048]{1,0:T(8,128)(2,1)}, u32[]{:S(2)}, u32[]{:S(2)}) collective-permute-start(bf16[768,2048]{1,0:T(8,128)(2,1)} %fusion.23), channel_id=1, source_target_pairs={{0,1},{1,2},{2,3},{3,0},{4,5},{5,6},{6,7},{7,4},{8,9},{9,10},{10,1... | collective-permute-start | bytes 9437192 | tf_op jit(solution)/shard_map/ppermute | solution.py:469
  1424.4 61.8 %collective-permute-start.24 = (bf16[768,2048]{1,0:T(8,128)(2,1)}, bf16[768,2048]{1,0:T(8,128)(2,1)}, u32[]{:S(2)}, u32[]{:S(2)}) collective-permute-start(bf16[768,2048]{1,0:T(8,128)(2,1)} %fusion.40), channel_id=1, source_target_pairs={{0,4},{4,0},{8,12},{12,8},{16,20},{20,16},{24,28},{28,24},{1,5},{5... | collective-permute-start | bytes 9437192 | tf_op jit(solution)/shard_map/ppermute | solution.py:459
  1486.2 71.1 %collective-permute-start.27 = (bf16[768,2048]{1,0:T(8,128)(2,1)}, bf16[768,2048]{1,0:T(8,128)(2,1)}, u32[]{:S(2)}, u32[]{:S(2)}) collective-permute-start(bf16[768,2048]{1,0:T(8,128)(2,1)} %fusion.24), channel_id=1, source_target_pairs={{0,1},{1,2},{2,3},{3,0},{4,5},{5,6},{6,7},{7,4},{8,9},{9,10},{10,1... | collective-permute-start | bytes 9437192 | tf_op jit(solution)/shard_map/ppermute | solution.py:469
  (98 other events, 1715.7 us)
Sparse Core Ops, SparseCore 0:
  12.5 60.9 all-gather.5
  227.8 53.6 all-gather.7
  283.4 113.7 all-gather.9
  398.9 113.7 all-gather.11
  534.7 115.2 all-gather.13
  770.9 129.0 reduce-scatter.9
  903.1 112.1 reduce-scatter.11
  1018.3 112.1 reduce-scatter.13
  1132.8 56.2 reduce-scatter.17
  1191.3 55.9 reduce-scatter.19
  1250.2 56.0 reduce-scatter.21
  1309.6 71.1 reduce-scatter.23
  1384.8 73.8 reduce-scatter.15
  1572.6 25.1 reduce-scatter.25

commit v3 on v2

--- a/solution.py
+++ b/solution.py
@@ -34,7 +34,7 @@
     return total
 
 
-PASS = dict(gram=3, inv=3, solve=3, state=3, out=3, back=3)
+PASS = dict(gram=3, inv=3, solve=3, state=3, out=3, back=3, side=1)
 
 
 def sigmoid(v):
@@ -267,17 +267,17 @@
             carried[h : h + 1, :] = flow * jnp.broadcast_to(
                 lane_sum(jnp.sum(dentry * entry, axis=0, keepdims=True)), (1, 128)
             )
-            dboth = mm(both, entry, NT, PASS["back"])
+            dboth = mm(both, entry, NT, PASS["side"])
             dq_decay, dw = dboth[:BLOCK], -dboth[BLOCK:]
-            dk_trail = mm(newest, ds, NT, PASS["back"])
-            dscores = mm(do, newest, NT, PASS["back"])
+            dk_trail = mm(newest, ds, NT, PASS["side"])
+            dscores = mm(do, newest, NT, PASS["side"])
             dright = mm(inverse, jnp.concatenate([dw, dnew], axis=1), TN, PASS["back"])
-            dsystem = -mm(dright, solved, NT, PASS["back"])
+            dsystem = -mm(dright, solved, NT, PASS["side"])
             dgram = jnp.concatenate(
                 [dscores * spread, jnp.where(row > col, dsystem * (b * spread), 0.0)], axis=0
             )
-            straight = mm(dgram, k, NN, PASS["back"])
-            across = mm(dgram, jnp.concatenate([q, k], axis=0), TN, PASS["back"])
+            straight = mm(dgram, k, NN, PASS["side"])
+            across = mm(dgram, jnp.concatenate([q, k], axis=0), TN, PASS["side"])
             dq = straight[:BLOCK] + dq_decay * p["eg"]
             dk = (
                 straight[BLOCK:] + across + dright[:, :HEAD_DIM] * beta_k + dk_trail * p["trail"]
@@ -339,11 +339,12 @@
     return pl.BlockSpec(shape, lambda i: (0,) * len(shape))
 
 
-def mixer_forward(z, offsets, lengths, params, carry, chunk, chunks, per_step=2):
+def mixer_forward(z, offsets, lengths, params, carry, chunk, chunks):
     rows, cols = z.shape
     heads = carry[0].shape[0]
     width = heads * HEAD_DIM
     blocks = rows // BLOCK // chunks
+    per_step = 4 if blocks % 4 == 0 else 2
     steps = blocks // per_step
     tile = per_step * BLOCK
     first = chunk * steps
@@ -384,12 +385,13 @@
 
 
 def mixer_backward(
-    z, offsets, lengths, params, dgated, saved, carry, chunk, chunks, per_step=2
+    z, offsets, lengths, params, dgated, saved, carry, chunk, chunks
 ):
     rows, cols = z.shape
     heads = carry[0].shape[0]
     width = heads * HEAD_DIM
     blocks = rows // BLOCK // chunks
+    per_step = 4 if blocks % 4 == 0 else 2
     steps = blocks // per_step
     tile = per_step * BLOCK
     last = chunk * steps + steps - 1

time: 1620 us -> 1610 us (level)
  transfers between devices with their start and end apart: 47 -> 47, of which waited for: 19 -> 19; matrix products, arithmetic and copies ran while one was open for 34% -> 34% of each run, Pallas kernels for 23% -> 22%
where the time goes in v3:
time: 1610 us; the launch traced here: 1600 us
  waiting for transfers between devices  483 us (30%)
  matrix products  428 us (27%)
  Pallas kernels  352 us (22%)
  local copies, waits for them, and re-layouts  184 us (11%)
  other arithmetic  79.4 us (5%)
  starting transfers between devices  56.5 us (4%)
    ppermute x18, waiting for transfers between devices, shift_tensor(): lax.ppermute(value, 'tensor', [(i, (i + distance) % size) for i in range(...  462 us
    pallas_call x4, Pallas kernels, mixer_backward(): pl.pallas_call(functools.partial(backward_kernel, per_step, heads, last),...  201 us
    dot_general x11, matrix products, project_rows(): lax.dot_general(left, weight, (((1,), (1,)), ((), ())), preferred_element...  156 us
    pallas_call x4, Pallas kernels, mixer_forward(): pl.pallas_call(functools.partial(forward_kernel, per_step, heads, first),...  151 us
    dot_general x5, matrix products, outer(): lax.dot_general(left, right, (((0,), (0,)), ((), ())), preferred_element_...  126 us
    dot_general x4, matrix products, per_device(): jnp.dot(shard, mixer_full, preferred_element_type=jnp.float32)  49.1 us
    ppermute x18, starting transfers between devices, shift_tensor(): lax.ppermute(value, 'tensor', [(i, (i + distance) % size) for i in range(...  49 us
    unnamed x162, local copies, waits for them, and re-layouts  47 us
  transfers between devices with their start and end apart: 47, of which 19 were waited for; matrix products, arithmetic and copies ran while one was open for 34% of the time, Pallas kernels for 22%

profile of v3, /device:TPU:0, one launch (start us, length us, event | category | flops | bytes accessed | tf_op | source)
XLA Modules:
  0.0 1597.9 jit_solution(11458805981256828316)
XLA Ops:
  22.3 39.3 %collective-permute-done = bf16[256,3328]{1,0:T(8,128)(2,1)} collective-permute-done((bf16[256,3328]{1,0:T(8,128)(2,1)S(1)}, bf16[256,3328]{1,0:T(8,128)(2,1)}, u32[]{:S(2)}, u32[]{:S(2)}) %collective-permute-start) | collective-permute-done | bytes 1703968 | tf_op jit(solution)/shard_map/ppermute | solution.py:471
  68.9 33.2 %collective-permute-done.1 = bf16[256,3328]{1,0:T(8,128)(2,1)} collective-permute-done((bf16[256,3328]{1,0:T(8,128)(2,1)}, bf16[256,3328]{1,0:T(8,128)(2,1)}, u32[]{:S(2)}, u32[]{:S(2)}) %collective-permute-start.1) | collective-permute-done | bytes 1703968 | tf_op jit(solution)/shard_map/ppermute | solution.py:471
  181.4 46.4 %collective-permute-done.3 = bf16[768,2048]{1,0:T(8,128)(2,1)} collective-permute-done((bf16[768,2048]{1,0:T(8,128)(2,1)}, bf16[768,2048]{1,0:T(8,128)(2,1)}, u32[]{:S(2)}, u32[]{:S(2)}) %collective-permute-start.3) | collective-permute-done | bytes 3145760 | tf_op jit(solution)/shard_map/ppermute | solution.py:471
  229.6 71.3 %collective-permute-done.6 = bf16[768,2048]{1,0:T(8,128)(2,1)} collective-permute-done((bf16[768,2048]{1,0:T(8,128)(2,1)}, bf16[768,2048]{1,0:T(8,128)(2,1)}, u32[]{:S(2)}, u32[]{:S(2)}) %collective-permute-start.6) | collective-permute-done | bytes 3145760 | tf_op jit(solution)/shard_map/ppermute | solution.py:471
  347.3 24.5 %collective-permute-done.7 = bf16[768,2048]{1,0:T(8,128)(2,1)} collective-permute-done((bf16[768,2048]{1,0:T(8,128)(2,1)}, bf16[768,2048]{1,0:T(8,128)(2,1)}, u32[]{:S(2)}, u32[]{:S(2)}) %collective-permute-start.7) | collective-permute-done | bytes 3145760 | tf_op jit(solution)/shard_map/ppermute | solution.py:471
  385.6 37.9 %mixer_forward.4 = (bf16[768,512]{1,0:T(8,128)(2,1)S(1)}, f32[768,512]{1,0:T(8,128)S(1)}, f32[12,4,128,128]{3,2,1,0:T(8,128)}, f32[768,512]{1,0:T(8,128)S(1)}, f...) custom-call(s32[1,3]{1,0:T(1,128)S(1)} %copy-done.5, s32[1,3]{1,0:T(1,128)S(1)} %copy-done.6, ...), custom_call_target="tpu_custom_call" | custom-call | tf_op jit(solution)/shard_map/mixer_forward/pallas_call | solution.py:354
  430.1 37.7 %mixer_forward.5 = (bf16[768,512]{1,0:T(8,128)(2,1)S(1)}, f32[768,512]{1,0:T(8,128)S(1)}, f32[12,4,128,128]{3,2,1,0:T(8,128)}, f32[768,512]{1,0:T(8,128)S(1)}, f...) custom-call(s32[1,3]{1,0:T(1,128)S(1)} %copy-done.5, s32[1,3]{1,0:T(1,128)S(1)} %copy-done.6, ...), custom_call_target="tpu_custom_call" | custom-call | tf_op jit(solution)/shard_map/mixer_forward/pallas_call | solution.py:354
  472.9 37.7 %mixer_forward.6 = (bf16[768,512]{1,0:T(8,128)(2,1)S(1)}, f32[768,512]{1,0:T(8,128)S(1)}, f32[12,4,128,128]{3,2,1,0:T(8,128)}, f32[768,512]{1,0:T(8,128)S(1)}, f...) custom-call(s32[1,3]{1,0:T(1,128)S(1)} %copy-done.5, s32[1,3]{1,0:T(1,128)S(1)} %copy-done.6, ...), custom_call_target="tpu_custom_call" | custom-call | tf_op jit(solution)/shard_map/mixer_forward/pallas_call | solution.py:354
  534.7 38.0 %mixer_forward.7 = (bf16[768,512]{1,0:T(8,128)(2,1)S(1)}, f32[768,512]{1,0:T(8,128)S(1)}, f32[12,4,128,128]{3,2,1,0:T(8,128)}, f32[768,512]{1,0:T(8,128)S(1)}, f...) custom-call(s32[1,3]{1,0:T(1,128)S(1)} %copy-done.5, s32[1,3]{1,0:T(1,128)S(1)} %copy-done.6, ...), custom_call_target="tpu_custom_call" | custom-call | tf_op jit(solution)/shard_map/mixer_forward/pallas_call | solution.py:354
  601.3 30.8 %collective-permute-done.13 = bf16[768,512]{1,0:T(8,128)(2,1)} collective-permute-done((bf16[768,512]{1,0:T(8,128)(2,1)}, bf16[768,512]{1,0:T(8,128)(2,1)}, u32[]{:S(2)}, u32[]{:S(2)}) %collective-permute-start.13) | collective-permute-done | bytes 786464 | tf_op jit(solution)/shard_map/ppermute | solution.py:471
  660.4 26.3 %fusion.39 = f32[1536,2816]{1,0:T(8,128)} fusion(bf16[2048,2816]{1,0:T(8,128)(2,1)} %all-gather.14.cloned.1.call-done, bf16[768,2048]{1,0:T(8,128)(2,1)} %collective-permute-done.16, bf16[768,2048]{1,0:T(8,128)(2,1)} %copy-done.50), kind=kOutput, calls=%fused_computation.67 | convolution fusion | flops 17729323008 | bytes 35127296 | tf_op jit(solution)/shard_map/dot_general | solution.py:689
  686.7 24.2 %fusion.70 = f32[1536,2816]{1,0:T(8,128)} fusion(bf16[1536,2048]{1,0:T(8,128)(2,1)S(1)} %copy-done.41, bf16[2048,2816]{1,0:T(8,128)(2,1)} %all-gather.12.cloned.1.call-done), kind=kOutput, calls=%fused_computation.183 | convolution fusion | flops 17716740096 | bytes 35127296 | tf_op jit(solution)/shard_map/dot_general | solution.py:690
  710.9 34.7 %multiply_convert_fusion.1 = (bf16[1536,2816]{1,0:T(8,128)(2,1)}, bf16[1536,2816]{1,0:T(8,128)(2,1)}, bf16[1536,2816]{1,0:T(8,128)(2,1)}) fusion(f32[1536,2816]{1,0:T(8,128)} %fusion.39, f32[1536,2816]{1,0:T(8,128)} %fusion.70, bf16[2048,2816]{1,0:T(8,128)(2,1)} %all-gather.10.cloned.1.call-done, bf16[768,2048]{1,0:T(8,128)(2,1)} %copy-done.49, ...), kind=kOutput, calls=%fused_computation.1 | convolution fusion | flops 17794203648 | bytes 78381056 | tf_op jit(solution)/shard_map/dot_general | solution.py:688
  745.6 24.4 %convolution_convert_fusion.2 = bf16[2048,2816]{1,0:T(8,128)(2,1)} fusion(bf16[1536,2816]{1,0:T(8,128)(2,1)} %get-tuple-element.282, bf16[768,2048]{1,0:T(8,128)(2,1)} %collective-permute-done.16, bf16[768,2048]{1,0:T(8,128)(2,1)} %copy-done.50), kind=kOutput, calls=%fused_computation.16 | convolution fusion | flops 17735090176 | bytes 26476544 | tf_op jit(solution)/shard_map/dot_general | solution.py:538
  878.8 24.8 %convolution_convert_fusion = bf16[2048,2816]{1,0:T(8,128)(2,1)} fusion(bf16[1536,2048]{1,0:T(8,128)(2,1)} %pad_maximum_fusion.1, bf16[1536,2816]{1,0:T(8,128)(2,1)} %get-tuple-element.349), kind=kOutput, calls=%fused_computation.14 | convolution fusion | flops 17722507264 | bytes 26476544 | tf_op jit(solution)/shard_map/dot_general | solution.py:538
  949.6 31.3 %collective-permute-done.19 = bf16[768,512]{1,0:T(8,128)(2,1)} collective-permute-done((bf16[768,512]{1,0:T(8,128)(2,1)}, bf16[768,512]{1,0:T(8,128)(2,1)}, u32[]{:S(2)}, u32[]{:S(2)}) %collective-permute-start.19) | collective-permute-done | bytes 786464 | tf_op jit(solution)/shard_map/ppermute | solution.py:471
  988.2 50.2 %mixer_backward.4 = (bf16[768,2176]{1,0:T(8,128)(2,1)}, f32[4,128,128]{2,1,0:T(8,128)S(1)}, f32[8,1536]{1,0:T(8,128)S(1)}, f32[8,128]{1,0:T(8,128)S(1)}, f32[4,8...) custom-call(s32[1,3]{1,0:T(1,128)S(1)} %copy-done.5, ...), custom_call_target="tpu_custom_call" | custom-call | flops 48000000000 | bytes 19200000 | tf_op jit(solution)/shard_map/mixer_backward/pallas_call | solution.py:402
  1058.6 50.3 %mixer_backward.5 = (bf16[768,2176]{1,0:T(8,128)(2,1)}, f32[4,128,128]{2,1,0:T(8,128)S(1)}, f32[8,1536]{1,0:T(8,128)S(1)}, f32[8,128]{1,0:T(8,128)S(1)}, f32[4,8...) custom-call(s32[1,3]{1,0:T(1,128)S(1)} %copy-done.5, ...), custom_call_target="tpu_custom_call" | custom-call | flops 48000000000 | bytes 19200000 | tf_op jit(solution)/shard_map/mixer_backward/pallas_call | solution.py:402
  1130.0 50.1 %mixer_backward.6 = (bf16[768,2176]{1,0:T(8,128)(2,1)}, f32[4,128,128]{2,1,0:T(8,128)S(1)}, f32[8,1536]{1,0:T(8,128)S(1)}, f32[8,128]{1,0:T(8,128)S(1)}, f32[4,8...) custom-call(s32[1,3]{1,0:T(1,128)S(1)} %copy-done.5, ...), custom_call_target="tpu_custom_call" | custom-call | flops 48000000000 | bytes 19200000 | tf_op jit(solution)/shard_map/mixer_backward/pallas_call | solution.py:402
  1230.6 50.3 %mixer_backward.7 = (bf16[768,2176]{1,0:T(8,128)(2,1)}, f32[4,128,128]{2,1,0:T(8,128)}, f32[8,1536]{1,0:T(8,128)}, f32[8,128]{1,0:T(8,128)}, f32[4,8,1536]{2,1,0...) custom-call(s32[1,3]{1,0:T(1,128)S(1)} %copy-done.5, s32[1,3]{1,0:T(1,128)S(1)} %copy-done.6, ...), custom_call_target="tpu_custom_call" | custom-call | flops 48000000000 | bytes 19200000 | tf_op jit(solution)/shard_map/mixer_backward/pallas_call | solution.py:402
  1317.7 41.3 %fusion.9 = bf16[2048,2176]{1,0:T(8,128)(2,1)} fusion(bf16[3072,2048]{1,0:T(8,128)(2,1)} %bitcast.223, bf16[768,2176]{1,0:T(8,128)(2,1)} %get-tuple-element.281, bf16[768,2176]{1,0:T(8,128)(2,1)} %get-tuple-element.280, bf16[768,2176]{1,0:T(8,128)(2,1)} %get-tuple-element.279, bf16[768,2176]{1,0:T(8,128)(2,1)} %get-tuple-element.278), kind=kOutput, calls=%fused_computation.17 | convolution fusion | flops 27438350336 | bytes 34865152 | tf_op jit(solution)/shard_map/dot_general | solution.py:538
  1359.2 27.1 %collective-permute-done.25 = bf16[768,2048]{1,0:T(8,128)(2,1)} collective-permute-done((bf16[768,2048]{1,0:T(8,128)(2,1)}, bf16[768,2048]{1,0:T(8,128)(2,1)}, u32[]{:S(2)}, u32[]{:S(2)}) %collective-permute-start.25) | collective-permute-done | bytes 3145760 | tf_op jit(solution)/shard_map/ppermute | solution.py:471
  1413.2 51.2 %collective-permute-done.26 = bf16[768,2048]{1,0:T(8,128)(2,1)} collective-permute-done((bf16[768,2048]{1,0:T(8,128)(2,1)}, bf16[768,2048]{1,0:T(8,128)(2,1)}, u32[]{:S(2)}, u32[]{:S(2)}) %collective-permute-start.26) | collective-permute-done | bytes 3145760 | tf_op jit(solution)/shard_map/ppermute | solution.py:471
  1489.8 51.6 %collective-permute-done.27 = bf16[768,2048]{1,0:T(8,128)(2,1)} collective-permute-done((bf16[768,2048]{1,0:T(8,128)(2,1)}, bf16[768,2048]{1,0:T(8,128)(2,1)}, u32[]{:S(2)}, u32[]{:S(2)}) %collective-permute-start.27) | collective-permute-done | bytes 3145760 | tf_op jit(solution)/shard_map/ppermute | solution.py:471
  (403 shorter events, 648.1 us)
Async XLA Ops:
  7.2 293.9 %all-gather.6.cloned.1.call-start = ((), (), s32[]{:S(2)}) async-start(), calls=%async_computation.9 | async-start | bytes 10027008 | tf_op jit(solution)/shard_map/all_gather | solution.py:624
  12.4 359.5 %all-gather.8.cloned.1.call-start = ((), (), s32[]{:S(2)}) async-start(), calls=%async_computation.10 | async-start | bytes 9437184 | tf_op jit(solution)/shard_map/all_gather | solution.py:645
  155.3 72.5 %collective-permute-start.3 = (bf16[768,2048]{1,0:T(8,128)(2,1)}, bf16[768,2048]{1,0:T(8,128)(2,1)}, u32[]{:S(2)}, u32[]{:S(2)}) collective-permute-start(bf16[768,2048]{1,0:T(8,128)(2,1)} %fusion.16), channel_id=1, source_target_pairs={{0,1},{1,2},{2,3},{3,0},{4,5},{5,6},{6,7},{7,4},{8,9},{9,10},{10,1... | collective-permute-start | bytes 9437192 | tf_op jit(solution)/shard_map/ppermute | solution.py:471
  227.8 202.3 %all-gather.10.cloned.1.call-start = ((), (), s32[]{:S(2)}) async-start(), calls=%async_computation.11 | async-start | bytes 14417920 | tf_op jit(solution)/shard_map/all_gather | solution.py:511
  228.6 305.6 %all-gather.12.cloned.1.call-start = ((), (), s32[]{:S(2)}) async-start(), calls=%async_computation.12 | async-start | bytes 14417920 | tf_op jit(solution)/shard_map/all_gather | solution.py:511
  229.1 431.3 %all-gather.14.cloned.1.call-start = ((), (), s32[]{:S(2)}) async-start(), calls=%async_computation.13 | async-start | bytes 14417920 | tf_op jit(solution)/shard_map/all_gather | solution.py:511
  229.2 71.7 %collective-permute-start.6 = (bf16[768,2048]{1,0:T(8,128)(2,1)}, bf16[768,2048]{1,0:T(8,128)(2,1)}, u32[]{:S(2)}, u32[]{:S(2)}) collective-permute-start(bf16[768,2048]{1,0:T(8,128)(2,1)} %collective-permute-done.3), channel_id=1, source_target_pairs={{0,1},{1,2},{2,3},{3,0},{4,5},{5,6},{6,7},{7,4},{8,9},{9,10},{10,1... | collective-permute-start | bytes 9437192 | tf_op jit(solution)/shard_map/ppermute | solution.py:471
  300.9 70.9 %collective-permute-start.7 = (bf16[768,2048]{1,0:T(8,128)(2,1)}, bf16[768,2048]{1,0:T(8,128)(2,1)}, u32[]{:S(2)}, u32[]{:S(2)}) collective-permute-start(bf16[768,2048]{1,0:T(8,128)(2,1)} %collective-permute-done.6), channel_id=1, source_target_pairs={{0,1},{1,2},{2,3},{3,0},{4,5},{5,6},{6,7},{7,4},{8,9},{9,10},{10,1... | collective-permute-start | bytes 9437192 | tf_op jit(solution)/shard_map/ppermute | solution.py:471
  371.8 55.2 %collective-permute-start.8 = (bf16[256,1408]{0,1:T(8,128)(2,1)S(1)}, bf16[256,1408]{0,1:T(8,128)(2,1)S(1)}, u32[]{:S(2)}, u32[]{:S(2)}) collective-permute-start(bf16[256,1408]{0,1:T(8,128)(2,1)S(1)} %copy.63), channel_id=1, source_target_pairs={{0,1},{1,2},{2,3},{3,0},{4,5},{5,6},{6,7},{7,4},{8,9},{9,10},{10,1... | collective-permute-start | bytes 2162696 | tf_op jit(solution)/shard_map/ppermute | solution.py:471
  534.2 504.2 %reduce-scatter.10.cloned.1.call-start = ((), (), s32[]{:S(2)}) async-start(), calls=%async_computation.14 | async-start | bytes 14417920 | tf_op jit(solution)/shard_map/reduce_scatter | solution.py:525
  770.0 338.9 %reduce-scatter.12.cloned.1.call-start = ((), (), s32[]{:S(2)}) async-start(), calls=%async_computation.15 | async-start | bytes 14417920 | tf_op jit(solution)/shard_map/reduce_scatter | solution.py:525
  878.7 301.4 %reduce-scatter.14.cloned.1.call-start = ((), (), s32[]{:S(2)}) async-start(), calls=%async_computation.16 | async-start | bytes 14417920 | tf_op jit(solution)/shard_map/reduce_scatter | solution.py:525
  903.6 507.3 %reduce-scatter.18.cloned.1.call-start = ((), (), s32[]{:S(2)}) async-start(), calls=%async_computation.18 | async-start | bytes 3604480 | tf_op jit(solution)/shard_map/reduce_scatter | solution.py:520
  925.1 55.8 %collective-permute-start.19 = (bf16[768,512]{1,0:T(8,128)(2,1)}, bf16[768,512]{1,0:T(8,128)(2,1)}, u32[]{:S(2)}, u32[]{:S(2)}) collective-permute-start(bf16[768,512]{1,0:T(8,128)(2,1)} %get-tuple-element.366), channel_id=1, source_target_pairs={{0,2},{1,3},{2,0},{3,1},{4,6},{5,7},{6,4},{7,5},{8,10},{9,11},{10,... | collective-permute-start | bytes 2359304 | tf_op jit(solution)/shard_map/ppermute | solution.py:471
  929.2 53.9 %collective-permute-start.20 = (bf16[768,512]{1,0:T(8,128)(2,1)S(1)}, bf16[768,512]{1,0:T(8,128)(2,1)}, u32[]{:S(2)}, u32[]{:S(2)}) collective-permute-start(bf16[768,512]{1,0:T(8,128)(2,1)S(1)} %get-tuple-element.365), channel_id=1, source_target_pairs={{0,3},{1,0},{2,1},{3,2},{4,7},{5,4},{6,5},{7,6},{8,11},{9,8},{10,9... | collective-permute-start | bytes 2359304 | tf_op jit(solution)/shard_map/ppermute | solution.py:471
  1055.5 432.0 %reduce-scatter.20.cloned.1.call-start = ((), (), s32[]{:S(2)}) async-start(), calls=%async_computation.19 | async-start | bytes 3604480 | tf_op jit(solution)/shard_map/reduce_scatter | solution.py:520
  1126.8 419.2 %reduce-scatter.22.cloned.1.call-start = ((), (), s32[]{:S(2)}) async-start(), calls=%async_computation.20 | async-start | bytes 3604480 | tf_op jit(solution)/shard_map/reduce_scatter | solution.py:520
  1197.0 357.2 %reduce-scatter.24.cloned.1.call-start = ((), (), s32[]{:S(2)}) async-start(), calls=%async_computation.21 | async-start | bytes 9437184 | tf_op jit(solution)/shard_map/reduce_scatter | solution.py:738
  1208.4 374.2 %reduce-scatter.16.cloned.1.call-start = ((), (), s32[]{:S(2)}) async-start(), calls=%async_computation.17 | async-start | bytes 10027008 | tf_op jit(solution)/shard_map/reduce_scatter | solution.py:746
  1302.3 84.0 %collective-permute-start.25 = (bf16[768,2048]{1,0:T(8,128)(2,1)}, bf16[768,2048]{1,0:T(8,128)(2,1)}, u32[]{:S(2)}, u32[]{:S(2)}) collective-permute-start(bf16[768,2048]{1,0:T(8,128)(2,1)} %dynamic-slice_bitcast_fusion), channel_id=1, source_target_pairs={{0,1},{1,2},{2,3},{3,0},{4,5},{5,6},{6,7},{7,4},{8,9},{9,10},{10,1... | collective-permute-start | bytes 9437192 | tf_op jit(solution)/shard_map/ppermute | solution.py:471
  1359.0 230.4 %reduce-scatter.26.cloned.1.call-start = ((), (), s32[]{:S(2)}) async-start(), calls=%async_computation.22 | async-start | bytes 1310720 | tf_op jit(solution)/shard_map/reduce_scatter | solution.py:520
  1392.6 71.8 %collective-permute-start.26 = (bf16[768,2048]{1,0:T(8,128)(2,1)}, bf16[768,2048]{1,0:T(8,128)(2,1)}, u32[]{:S(2)}, u32[]{:S(2)}) collective-permute-start(bf16[768,2048]{1,0:T(8,128)(2,1)} %fusion.23), channel_id=1, source_target_pairs={{0,1},{1,2},{2,3},{3,0},{4,5},{5,6},{6,7},{7,4},{8,9},{9,10},{10,1... | collective-permute-start | bytes 9437192 | tf_op jit(solution)/shard_map/ppermute | solution.py:471
  1410.7 59.8 %collective-permute-start.24 = (bf16[768,2048]{1,0:T(8,128)(2,1)}, bf16[768,2048]{1,0:T(8,128)(2,1)}, u32[]{:S(2)}, u32[]{:S(2)}) collective-permute-start(bf16[768,2048]{1,0:T(8,128)(2,1)} %fusion.40), channel_id=1, source_target_pairs={{0,4},{4,0},{8,12},{12,8},{16,20},{20,16},{24,28},{28,24},{1,5},{5... | collective-permute-start | bytes 9437192 | tf_op jit(solution)/shard_map/ppermute | solution.py:461
  1470.5 70.8 %collective-permute-start.27 = (bf16[768,2048]{1,0:T(8,128)(2,1)}, bf16[768,2048]{1,0:T(8,128)(2,1)}, u32[]{:S(2)}, u32[]{:S(2)}) collective-permute-start(bf16[768,2048]{1,0:T(8,128)(2,1)} %fusion.24), channel_id=1, source_target_pairs={{0,1},{1,2},{2,3},{3,0},{4,5},{5,6},{6,7},{7,4},{8,9},{9,10},{10,1... | collective-permute-start | bytes 9437192 | tf_op jit(solution)/shard_map/ppermute | solution.py:471
  (98 other events, 1716.8 us)
Sparse Core Ops, SparseCore 0:
  12.5 60.9 all-gather.5
  227.9 53.6 all-gather.7
  283.5 113.7 all-gather.9
  399.0 113.8 all-gather.11
  534.3 115.1 all-gather.13
  770.1 129.0 reduce-scatter.9
  902.3 112.0 reduce-scatter.11
  1017.6 112.1 reduce-scatter.13
  1132.0 56.1 reduce-scatter.17
  1190.4 56.0 reduce-scatter.19
  1249.3 56.0 reduce-scatter.21
  1308.8 71.0 reduce-scatter.23
  1383.9 73.8 reduce-scatter.15
  1556.6 25.0 reduce-scatter.25
